TPU v7x, 32 devices: a whole 2x2x4 slice. The times are simulated.
32 devices in a mesh: ep: 16 (over z, x, core), tp: 2 (over y).
Axes of the slice: x: 2, y: 2, z: 4, core: 2. Of those that a mesh axis runs over, the one named last changes fastest.
Arguments:
- hidden_in: bfloat16 [2048, 2048], P('ep', 'tp'), may hold values from -50 to 50
- norm_gain: float32 [2048], P('tp'), may hold values from 0.5 to 1.5
- expert_ids: int32 [2048, 8], P('ep'), may hold values from 0 to 31, all different within a row; in each aligned block of 128 rows (0 to 127, 128 to 255, ...) at most 48 rows name the same one
- routing_weight: float32 [2048, 8], P('ep'), may hold values from 0.03 to 0.3
- labels: int32 [2048], P('ep'), may hold values from 0 to 3
- grad_later: bfloat16 [2048, 2048], P('ep', 'tp'), may hold values from -6 to 6
- head_weight: bfloat16 [2048, 4], P('tp'), may hold values from -0.125 to 0.125
- gate_weight: bfloat16 [24576, 2048], P(('ep', 'tp')), may hold values from -0.125 to 0.125
- up_weight: bfloat16 [24576, 2048], P(('ep', 'tp')), may hold values from -0.125 to 0.125
- down_weight: bfloat16 [24576, 2048], P(('ep', 'tp')), may hold values from -0.21875 to 0.21875
Outputs:
- token_loss: float32 [2048], P('ep')
- outcome: bfloat16 [2048, 2048], P('ep', 'tp')
- grad_input: bfloat16 [2048, 2048], P('ep', 'tp')
- grad_gate: bfloat16 [24576, 2048], P(('ep', 'tp'))
- grad_up: bfloat16 [24576, 2048], P(('ep', 'tp'))
- grad_down: bfloat16 [24576, 2048], P(('ep', 'tp'))
Inputs may be any that keep to these rules, and one draw needn't show every extreme that they name: `expert_ids`: each row names 8 different experts. Within the 128 rows of one index of ep, no expert is named more than 48 times, a bound that some block reaches.
All inputs are finite; a program needn't handle non-finite values.
Results may differ from a plain program's by a relative error of at most 0.011.
Values may be sent and summed in bfloat16 or wider, within the bound.
No kernel may reach another device: no remote copies, remote signals or barrier semaphores. Data moves between devices by JAX's collectives and lax.ppermute only.
A program may use at most 128 MiB of HBM per device.

v0:
```python
import functools

import jax
import jax.numpy as jnp
from jax import lax
from jax.experimental import pallas as pl
from jax.experimental.pallas import tpu as pltpu
from jax.sharding import PartitionSpec as P

FF = 768

EPS = 1e-06
LOSS_SCALE = 64.0
BF = jnp.bfloat16
F32 = jnp.float32
EXACT = lax.Precision.HIGHEST
VMEM_BYTES = 24 * 1024 * 1024
LANES = 128


def ring_sizes(dev_count):
    chips = dev_count // 2
    across = 1
    while across * across * 4 <= chips:
        across *= 2
    return across, chips // across


def send(value, target):
    dev_count, tp = lax.axis_size("ep"), lax.axis_size("tp")
    pairs = []
    for i in range(dev_count):
        for j in range(tp):
            a, b = target(i, j)
            pairs.append((i * tp + j, a * tp + b))
    return lax.ppermute(value, ("ep", "tp"), pairs)


def send_z(value, k, across):
    return send(value, lambda i, j: (i ^ (2 * across * k), j))


def send_core(value):
    return send(value, lambda i, j: (i ^ 1, j))


def send_x(value, k):
    return send(value, lambda i, j: (i ^ (2 * k), j))


def send_y(value, k):
    return send(value, lambda i, j: (i, j ^ k))


def send_first(value, k):
    return send(value, lambda i, j: (i, j ^ k) if i % 2 else (i ^ (2 * k), j))


def send_last(value, k):
    return send(value, lambda i, j: (i ^ (2 * k), j) if i % 2 else (i, j ^ k))


def xor_blocks(value, axis, index):
    size = value.shape[axis]
    bit = 1
    while bit < size:
        shape = value.shape
        split = shape[:axis] + (size // (2 * bit), 2, bit) + shape[axis + 1 :]
        pairs = value.reshape(split)
        turned = jnp.flip(pairs, axis + 1)
        value = jnp.where((index & bit) > 0, turned, pairs).reshape(shape)
        bit *= 2
    return value


def params():
    return pltpu.CompilerParams(vmem_limit_bytes=VMEM_BYTES)


def whole_spec(shape):
    return pl.BlockSpec(shape, lambda *_: (0,) * len(shape))


def selector(pos_ref, h, cap, experts, tokens):
    slots = lax.broadcasted_iota(jnp.int32, (cap, tokens), 0).astype(F32)
    parts = [
        jnp.where(pos_ref[h, 0, e : e + 1, :] == slots, 1.0, 0.0).astype(F32) for e in range(experts)
    ]
    return jnp.concatenate(parts, axis=0).astype(BF)


def pick_rows(units, pos, start, cap):
    n = len(units)
    group, tokens, width = units[0].shape
    experts = pos.shape[2]

    def body(*refs):
        pos_ref, ins, outs = refs[0], refs[1 : 1 + n], refs[1 + n :]
        for h in range(n):
            chosen = selector(pos_ref, h, cap, experts, tokens)
            rows = jnp.dot(chosen, ins[h][0], preferred_element_type=F32).astype(BF)
            for e in range(experts):
                outs[e][h, 0] = rows[e * cap : (e + 1) * cap]

    return pl.pallas_call(
        body,
        grid=(group,),
        in_specs=[pl.BlockSpec((n, 1, experts, tokens), lambda z: (0, z + start, 0, 0))]
        + [pl.BlockSpec((1, tokens, width), lambda z: (z, 0, 0))] * n,
        out_specs=[pl.BlockSpec((n, 1, cap, width), lambda z: (0, z, 0, 0))] * experts,
        out_shape=[jax.ShapeDtypeStruct((n, group, cap, width), BF)] * experts,
        compiler_params=params(),
        cost_estimate=pl.CostEstimate(
            flops=2 * group * n * experts * cap * tokens * width,
            bytes_accessed=2 * group * n * width * (tokens + experts * cap),
            transcendentals=0,
        ),
        name="pick_rows",
    )(pos, *units)


def spread_rows(sources, pos, start, group, cap, width):
    n, _, experts, tokens = pos.shape

    def body(*refs):
        pos_ref, ins, outs = refs[0], refs[1 : 1 + experts], refs[1 + experts :]
        for h in range(n):
            chosen = selector(pos_ref, h, cap, experts, tokens)
            rows = jnp.concatenate(
                [ref[(0,) * len(prefix) + (h, 0)] for ref, (_, prefix) in zip(ins, sources)], axis=0
            )
            dense = lax.dot_general(chosen, rows, (((0,), (0,)), ((), ())), preferred_element_type=F32)
            outs[h][0] = dense.astype(BF)

    def spec(prefix):
        return pl.BlockSpec((1,) * len(prefix) + (n, 1, cap, width), lambda z: prefix + (0, z, 0, 0))

    return pl.pallas_call(
        body,
        grid=(group,),
        in_specs=[pl.BlockSpec((n, 1, experts, tokens), lambda z: (0, z + start, 0, 0))]
        + [spec(prefix) for _, prefix in sources],
        out_specs=[pl.BlockSpec((1, tokens, width), lambda z: (z, 0, 0))] * n,
        out_shape=[jax.ShapeDtypeStruct((group, tokens, width), BF)] * n,
        compiler_params=params(),
        cost_estimate=pl.CostEstimate(
            flops=2 * group * n * experts * cap * tokens * width,
            bytes_accessed=2 * group * n * width * (tokens + experts * cap),
            transcendentals=0,
        ),
        name="spread_rows",
    )(pos, *[array for array, _ in sources])


def assemble(place, pieces, groups, finish, extra, extra_specs, model_width, name):
    n = len(pieces[0][0])
    _, _, cap, width = pieces[0][0][0].shape
    depth = sum(len(g) for g in groups)
    count = len(groups) * 2 * n

    def body(place_ref, *refs):
        ins, more, out_ref = refs[:count], refs[count:-1], refs[-1]
        z = pl.program_id(0)
        core, col = place_ref[0], place_ref[1]

        def fill(g):
            for cr in range(2):
                kind = core ^ cr
                for f in range(n):
                    ref = ins[(g * 2 + cr) * n + f]
                    for h in range(n):
                        x = jnp.where(kind == 0, h, f)
                        y = jnp.where(kind == 0, f, h) ^ col
                        lanes = pl.ds(pl.multiple_of(y * width, LANES), width)
                        out_ref[0, cr * n + x, :, lanes] = ref[h, 0]

        for g, members in enumerate(groups):
            if len(groups) == 1:
                fill(g)
            else:
                pl.when(jnp.logical_and(z >= members[0], z <= members[-1]))(functools.partial(fill, g))
        for b in range(2 * n):
            out_ref[0, b] = finish(b, out_ref[0, b].astype(F32), *more)

    def piece_spec(members):
        first, last = members[0], members[-1]
        return pl.BlockSpec(
            (n, 1, cap, width), lambda z, *_: (0, jnp.clip(z, first, last) - first, 0, 0)
        )

    in_specs = [piece_spec(members) for members in groups for _ in range(2 * n)]
    flat = [piece for group in pieces for side in group for piece in side]
    return pl.pallas_call(
        body,
        grid_spec=pltpu.PrefetchScalarGridSpec(
            num_scalar_prefetch=1,
            grid=(depth,),
            in_specs=in_specs + extra_specs,
            out_specs=pl.BlockSpec((1, 2 * n, cap, model_width), lambda z, *_: (z, 0, 0, 0)),
        ),
        out_shape=jax.ShapeDtypeStruct((depth, 2 * n, cap, model_width), BF),
        compiler_params=params(),
        cost_estimate=pl.CostEstimate(
            flops=10 * depth * 2 * n * cap * model_width,
            bytes_accessed=4 * depth * 2 * n * cap * model_width,
            transcendentals=0,
        ),
        name=name,
    )(place, *flat, *extra)


def column_product(place, terms, scale, groups, depth, n, cap, width, name):
    count = len(terms)
    units = terms[0][0].shape[1]

    def where_to(y, b, place_ref):
        cr, x = b // n, b % n
        kind = place_ref[0] ^ cr
        y_rel = y ^ place_ref[1]
        return cr, jnp.where(kind == 0, y_rel, x), jnp.where(kind == 0, x, y_rel)

    def body(place_ref, *refs):
        total = None
        for i in range(count):
            left = refs[2 * i][...].reshape(depth * cap, units)
            term = jnp.dot(left, refs[2 * i + 1][...], preferred_element_type=F32)
            total = term if total is None else total + term
        rest = refs[2 * count :]
        if scale is not None:
            total = total * rest[0][...].reshape(depth * cap, LANES)[:, :1]
            rest = rest[1:]
        rows = total.astype(BF).reshape(depth, cap, width)
        for ref, members in zip(rest, groups):
            ref[0, 0, 0] = rows[members[0] : members[-1] + 1]

    left_spec = pl.BlockSpec((depth, 1, cap, units), lambda y, b, *_: (0, b, 0, 0))
    in_specs, args = [], []
    for left, right in terms:
        in_specs += [left_spec, pl.BlockSpec((units, width), lambda y, b, *_: (0, y))]
        args += [left.reshape(depth, 2 * n, cap, units), right]
    if scale is not None:
        in_specs.append(pl.BlockSpec((depth, 1, cap, LANES), lambda y, b, *_: (0, b, 0, 0)))
        args.append(scale)
    return pl.pallas_call(
        body,
        grid_spec=pltpu.PrefetchScalarGridSpec(
            num_scalar_prefetch=1,
            grid=(n, 2 * n),
            in_specs=in_specs,
            out_specs=[
                pl.BlockSpec(
                    (1, 1, 1, len(members), cap, width),
                    lambda y, b, place_ref: where_to(y, b, place_ref) + (0, 0, 0),
                )
                for members in groups
            ],
        ),
        out_shape=[
            jax.ShapeDtypeStruct((2, n, n, len(members), cap, width), BF) for members in groups
        ],
        compiler_params=params(),
        cost_estimate=pl.CostEstimate(
            flops=2 * count * depth * 2 * n * cap * units * width * n,
            bytes_accessed=2 * count * (units * width * n + depth * 2 * n * cap * units)
            + 2 * depth * 2 * n * cap * width * n,
            transcendentals=0,
        ),
        name=name,
    )(place, *args)


def own_selector(pos_ref, b, cap, tokens):
    slots = lax.broadcasted_iota(jnp.int32, (cap, tokens), 0).astype(F32)
    return jnp.where(pos_ref[0, b] == slots, 1.0, 0.0).astype(BF)


def row_sums(active, down_head, pos_own, weight_parts, labels, depth, n, cap):
    units = active.shape[1]
    tokens = pos_own.shape[-1]

    def body(active_ref, head_ref, pos_ref, weight_ref, out_ref, scale_ref):
        for b in range(2 * n):
            chosen = own_selector(pos_ref, b, cap, tokens)
            parts = lax.dot_general(
                chosen, weight_ref[0, b], (((1,), (1,)), ((), ())), preferred_element_type=F32
            )
            scale = parts[:, 0:1] + parts[:, 1:2] + parts[:, 2:3]
            scale_ref[0, b] = jnp.broadcast_to(scale, (cap, LANES))
            rows = jnp.dot(active_ref[0, b], head_ref[...], preferred_element_type=F32) * scale
            high = rows.astype(BF)
            low = (rows - high.astype(F32)).astype(BF)
            dense = lax.dot_general(
                high, chosen, (((0,), (0,)), ((), ())), preferred_element_type=F32
            ) + lax.dot_general(low, chosen, (((0,), (0,)), ((), ())), preferred_element_type=F32)
            out_ref[0, b] = dense[0:labels] + dense[8 : 8 + labels]

    return pl.pallas_call(
        body,
        grid=(depth,),
        in_specs=[
            pl.BlockSpec((1, 2 * n, cap, units), lambda z: (z, 0, 0, 0)),
            whole_spec((units, LANES)),
            pl.BlockSpec((1, 2 * n, 1, tokens), lambda z: (z, 0, 0, 0)),
            pl.BlockSpec((1, 2 * n, 16, tokens), lambda z: (z, 0, 0, 0)),
        ],
        out_specs=[
            pl.BlockSpec((1, 2 * n, labels, tokens), lambda z: (z, 0, 0, 0)),
            pl.BlockSpec((1, 2 * n, cap, LANES), lambda z: (z, 0, 0, 0)),
        ],
        out_shape=[
            jax.ShapeDtypeStruct((depth, 2 * n, labels, tokens), F32),
            jax.ShapeDtypeStruct((depth, 2 * n, cap, LANES), F32),
        ],
        compiler_params=params(),
        cost_estimate=pl.CostEstimate(
            flops=2 * depth * 2 * n * cap * units * LANES,
            bytes_accessed=2 * depth * 2 * n * cap * (units + 256),
            transcendentals=0,
        ),
        name="row_sums",
    )(active.reshape(depth, 2 * n, cap, units), down_head, pos_own, weight_parts)


def gather_rows(value, pos, groups, across, cap, column=None):
    depth = sum(len(g) for g in groups)
    n = across
    if column is None:
        column = [value] + [send_z(value, k, across) for k in range(1, depth)]
    pieces = []
    for members in groups:
        stacked = jnp.stack([column[k] for k in members])
        units = [stacked] + [send_first(stacked, k) for k in range(1, n)]
        rows = pick_rows(units, pos, members[0], cap)
        here, other = [], []
        for f in range(n):
            same, cross = rows[2 * f], rows[2 * f + 1]
            if f > 0:
                cross = send_last(cross, f)
                same = send_last(same, f)
            here.append(same)
            other.append(send_core(cross))
        pieces.append([here, other])
    return pieces


def return_rows(rows, pos, groups, across, cap):
    n = across
    width = rows[0].shape[-1]
    column = {}
    for g in reversed(range(len(groups))):
        members = groups[g]
        mine = rows[g]
        crossed = send_core(mine[1])
        sources = [(mine, (0, 0)), (crossed, (0,))]
        for f in range(1, n):
            sources += [(send_last(mine[0, f], f), ()), (send_last(crossed[f], f), ())]
        dense = spread_rows(sources, pos, members[0], len(members), cap, width)
        total = dense[0].astype(F32)
        for h in range(1, n):
            total = total + send_first(dense[h], h).astype(F32)
        for i, k in enumerate(members):
            column[k] = total[i]
    result = column[0]
    for k in sorted(column, reverse=True):
        if k > 0:
            result = result + send_z(column[k].astype(BF), k, across).astype(F32)
    return result


def sum_all(value):
    step = 1
    while step < lax.axis_size("ep"):
        value = value + send(value, lambda i, j: (i ^ step, j))
        step *= 2
    step = 1
    while step < lax.axis_size("tp"):
        value = value + send_y(value, step)
        step *= 2
    return value


def split_bf(value, parts):
    pieces = []
    for _ in range(parts):
        piece = value.astype(BF)
        pieces.append(piece)
        value = value - piece.astype(F32)
    return pieces


def shards(
    hidden_in,
    norm_gain,
    expert_ids,
    routing_weight,
    labels,
    grad_later,
    head_weight,
    gate_weight,
    up_weight,
    down_weight,
):
    dev_count = lax.axis_size("ep")
    n = lax.axis_size("tp")
    row, col = lax.axis_index("ep"), lax.axis_index("tp")
    core = row & 1
    across, depth = ring_sizes(dev_count)
    if across != n:
        raise ValueError("x and y differ")
    tok_count, width = hidden_in.shape
    top_count = expert_ids.shape[1]
    model_width = gate_weight.shape[1]
    unit_rows = gate_weight.shape[0]
    local_count = unit_rows * n // FF
    expert_count = local_count * dev_count
    capacity = tok_count * top_count * 3 // (2 * expert_count)
    cap = -(-capacity // 16) * 16
    row_count = dev_count * cap
    label_count = head_weight.shape[1]
    place = jnp.stack([core, col]).astype(jnp.int32)
    two = [tuple(range(depth // 2)), tuple(range(depth // 2, depth))]
    one = [tuple(range(depth))]

    def expert_of(ep_index, tp_index):
        return ep_index * local_count + tp_index * unit_rows // FF

    spare = -(2 * top_count + 1) % 8
    meta = jnp.concatenate(
        [
            expert_ids.T.astype(F32),
            routing_weight.T,
            labels.astype(F32)[None, :],
            jnp.zeros((spare, tok_count), F32),
        ]
    )
    meta = jnp.stack([meta] + [send_z(meta, k, across) for k in range(1, depth)])
    meta = jnp.stack([meta] + [send_x(meta, k) for k in range(1, n)], axis=1)
    meta = jnp.stack([meta, send_core(meta)], axis=1)

    feature_rows = jnp.concatenate(
        [
            norm_gain[None, :],
            head_weight.astype(F32).T,
            jnp.zeros((-(1 + label_count) % 8, width), F32),
        ]
    )
    own_gain, own_head = feature_rows[0], feature_rows[1 : 1 + label_count]
    all_features = jnp.stack([feature_rows] + [send_y(feature_rows, j) for j in range(1, n)], axis=1)
    all_features = xor_blocks(all_features, 1, col).reshape(feature_rows.shape[0], model_width)

    hidden_column = [hidden_in] + [send_z(hidden_in, k, across) for k in range(1, depth)]

    spot = jnp.arange(tok_count, dtype=jnp.int32)
    earlier = (spot[:, None] < spot[None, :]).astype(BF)

    def positions(ids, experts):
        member = jnp.stack([jnp.sum((ids == e.astype(F32)).astype(F32), axis=-2) for e in experts], axis=-2)
        before = lax.dot_general(
            member.astype(BF), earlier, (((member.ndim - 1,), (0,)), ((), ())), preferred_element_type=F32
        )
        return jnp.where(member > 0, before, -1.0)

    ids = meta[..., :top_count, :]
    near = [expert_of(row, col), expert_of(row ^ 1, col)]
    for f in range(1, n):
        far_row = jnp.where(core == 0, row, row ^ (2 * f))
        far_col = jnp.where(core == 0, col ^ f, col)
        near += [expert_of(far_row, far_col), expert_of(far_row ^ 1, far_col)]
    unit_ids = jnp.stack([jnp.where(core == 0, ids[:, 0, h], ids[:, 0, 0]) for h in range(n)])
    pos = positions(unit_ids, near)
    blocks = ids.reshape(depth, 2 * n, top_count, tok_count)
    pos_own = positions(blocks, [expert_of(row, col)])
    named_own = (blocks == expert_of(row, col).astype(F32)).astype(F32)
    weights = meta[..., top_count : 2 * top_count, :].reshape(blocks.shape)
    weight_own = jnp.sum(named_own * weights, axis=-2, keepdims=True)
    blank = jnp.zeros((depth, 2 * n, 13, tok_count), BF)
    weight_parts = jnp.concatenate(split_bf(weight_own, 3) + [blank], axis=2)
    label_all = meta[..., 2 * top_count, :]

    hidden_wide = hidden_in.astype(F32)
    own_squares = jnp.sum(hidden_wide * hidden_wide, axis=1)
    squares = own_squares
    for j in range(1, n):
        squares = squares + send_y(own_squares, j)
    inv_rms = lax.rsqrt(squares / model_width + EPS)[:, None]

    head_pair = jnp.concatenate([all_features[1:], jnp.zeros((1, model_width), F32)])
    head_pad = jnp.concatenate(
        [head_pair, head_pair, jnp.zeros((LANES - 16, model_width), F32)]
    ).astype(BF)
    down_head = lax.dot_general(
        down_weight, head_pad, (((1,), (1,)), ((), ())), preferred_element_type=F32
    )
    high = down_head.astype(BF)
    lane = lax.broadcasted_iota(jnp.int32, down_head.shape, 1)
    down_head = jnp.where(lane < 8, high, (down_head - high.astype(F32)).astype(BF))

    pieces = gather_rows(hidden_in, pos, two, across, cap, hidden_column)

    def normed(b, value, features_ref):
        rms = lax.rsqrt(jnp.sum(value * value, axis=1, keepdims=True) / model_width + EPS)
        return (value * rms * features_ref[0:1, :]).astype(BF)

    received = assemble(
        place, pieces, two, normed, [all_features], [whole_spec(all_features.shape)], model_width, "normed_rows"
    ).reshape(row_count, model_width)

    later_in = lax.optimization_barrier([grad_later] + hidden_column)[0]
    later = gather_rows(later_in, pos, one, across, cap)

    def against(left, right):
        return lax.dot_general(left, right, (((1,), (1,)), ((), ())), preferred_element_type=F32)

    def over_rows(left, right):
        return lax.dot_general(left, right, (((0,), (0,)), ((), ())), preferred_element_type=F32).astype(BF)

    gate_pre = against(received, gate_weight)
    up_pre = against(received, up_weight)
    sigma = jax.nn.sigmoid(gate_pre)
    active = (gate_pre * sigma * up_pre).astype(BF)

    logits, scale = row_sums(active, down_head, pos_own, weight_parts, label_count, depth, n, cap)
    own_logits = lax.dot_general(
        own_head.astype(BF), hidden_in, (((1,), (1,)), ((), ())), preferred_element_type=F32
    )

    def turn(value):
        value = value.reshape((depth, 2, n) + value.shape[-2:])
        value = xor_blocks(value, 0, row // (2 * across))
        value = xor_blocks(value, 1, core)
        return xor_blocks(value, 2, (row // 2) & (across - 1))

    block = jnp.arange(depth * 2 * n).reshape(depth, 2 * n)
    logits = logits + jnp.where((block == 0)[..., None, None], own_logits, 0.0)
    logits = turn(sum_all(turn(logits)))
    classes = (label_all[..., None, :] == jnp.arange(label_count, dtype=F32)[:, None]).astype(F32)
    powers = jnp.exp(logits)
    totals = jnp.sum(powers, axis=-2, keepdims=True)
    d_logits = (powers / totals - classes) * LOSS_SCALE
    token_loss = jnp.log(totals[0, 0, 0, 0]) - jnp.sum(logits[0, 0, 0] * classes[0, 0, 0], axis=0)

    d_parts = jnp.concatenate(
        split_bf(d_logits.reshape(depth, 2 * n, label_count, tok_count), 2)
        + [weight_parts[:, :, : 16 - 2 * label_count]],
        axis=2,
    )

    def gradient_rows(b, value, features_ref, pos_ref, parts_ref):
        chosen = own_selector(pos_ref, b, cap, tok_count)
        parts = lax.dot_general(
            chosen, parts_ref[0, b], (((1,), (1,)), ((), ())), preferred_element_type=F32
        )
        for k in range(label_count):
            d_logit = parts[:, k : k + 1] + parts[:, label_count + k : label_count + k + 1]
            value = value + d_logit * features_ref[1 + k : 2 + k, :]
        first = 2 * label_count
        weight = parts[:, first : first + 1] + parts[:, first + 1 : first + 2] + parts[:, first + 2 : first + 3]
        return (value.astype(BF).astype(F32) * weight).astype(BF)

    grads_in = assemble(
        place,
        later,
        one,
        gradient_rows,
        [all_features, pos_own, d_parts],
        [
            whole_spec(all_features.shape),
            pl.BlockSpec((1, 2 * n, 1, tok_count), lambda z, *_: (z, 0, 0, 0)),
            pl.BlockSpec((1, 2 * n, 16, tok_count), lambda z, *_: (z, 0, 0, 0)),
        ],
        model_width,
        "gradient_rows",
    ).reshape(row_count, model_width)

    d_active = against(grads_in, down_weight)
    d_gate = (d_active * up_pre * sigma * (1.0 + gate_pre * (1.0 - sigma))).astype(BF)
    d_up = (d_active * gate_pre * sigma).astype(BF)

    d_rows = column_product(
        place, [(d_gate, gate_weight), (d_up, up_weight)], None, two, depth, n, cap, width, "d_rows"
    )
    d_normed = return_rows(d_rows, pos, two, across, cap)
    out_rows = column_product(
        place, [(active, down_weight)], scale, one, depth, n, cap, width, "out_rows"
    )
    mixed = return_rows(out_rows, pos, one, across, cap)

    grad_down = over_rows(active, grads_in)
    grad_gate = over_rows(d_gate, received)
    grad_up = over_rows(d_up, received)

    outcome = (hidden_wide + mixed).astype(BF)
    d_outcome = lax.dot_general(
        d_logits[0, 0, 0], own_head, (((0,), (0,)), ((), ())), precision=EXACT
    ) + grad_later.astype(F32)
    d_scaled = d_normed * own_gain[None, :]
    products = jnp.sum(d_scaled * hidden_wide, axis=1)
    slope = products
    for j in range(1, n):
        slope = slope + send_y(products, j)
    slope = slope[:, None] / model_width
    d_hidden = inv_rms * d_scaled - hidden_wide * (inv_rms * inv_rms * inv_rms) * slope
    grad_input = (d_outcome + d_hidden).astype(BF)
    return token_loss, outcome, grad_input, grad_gate, grad_up, grad_down


def solution(mesh):
    in_specs = (
        P("ep", "tp"),
        P("tp"),
        P("ep", None),
        P("ep", None),
        P("ep"),
        P("ep", "tp"),
        P("tp", None),
        P(("ep", "tp"), None),
        P(("ep", "tp"), None),
        P(("ep", "tp"), None),
    )
    out_specs = (
        P("ep"),
        P("ep", "tp"),
        P("ep", "tp"),
        P(("ep", "tp"), None),
        P(("ep", "tp"), None),
        P(("ep", "tp"), None),
    )
    return jax.shard_map(shards, mesh=mesh, in_specs=in_specs, out_specs=out_specs, check_vma=False)
```

profile of v0, /device:TPU:0, one launch (start us, length us, event | category | flops | bytes accessed | tf_op | source)
XLA Modules:
  0.0 238.5 jit_solution(5293380251304600498)
XLA Ops:
  2.8 4.0 %collective-permute-start.1 = (f32[24,128]{1,0:T(8,128)S(1)}, f32[24,128]{1,0:T(8,128)S(1)}, u32[]{:S(2)}, u32[]{:S(2)}) collective-permute-start(f32[24,128]{1,0:T(8,128)S(1)} %get-tuple-element.83), channel_id=1, source_target_pairs={{0,16},{1,17},{2,18},{3,19},{4,20},{5,21},{6,22},{7,23},{8,24},{9,... | collective-permute-start | bytes 36872 | tf_op jit(solution)/shard_map/ppermute | solution.py:36
  8.4 3.8 %collective-permute-start.11 = (bf16[128,1024]{1,0:T(8,128)(2,1)}, bf16[128,1024]{1,0:T(8,128)(2,1)S(1)}, u32[]{:S(2)}, u32[]{:S(2)}) collective-permute-start(bf16[128,1024]{1,0:T(8,128)(2,1)} %param.10), channel_id=1, source_target_pairs={{0,24},{1,25},{2,26},{3,27},{4,28},{5,29},{6,30},{7,31},{8,16},{9,... | collective-permute-start | bytes 786440 | tf_op jit(solution)/shard_map/ppermute | solution.py:36
  20.0 2.9 %fusion.14.head_ref = bf16[768,128]{1,0:T(8,128)(2,1)S(1)} fusion(bf16[128,2048]{1,0:T(8,128)(2,1)S(1)} %concatenate.20, bf16[768,2048]{1,0:T(8,128)(2,1)} %refs_1_.2, pred[128]{0:T(512)(128)(4,1)S(1)} %iota_compare_fusion.3), kind=kOutput, calls=%fused_computation.48 | convolution fusion | flops 403144704 | bytes 3866752 | tf_op jit(solution)/shard_map/dot_general | solution.py:491
  23.1 10.3 %collective-permute-done.10 = bf16[128,1024]{1,0:T(8,128)(2,1)S(1)} collective-permute-done((bf16[128,1024]{1,0:T(8,128)(2,1)}, bf16[128,1024]{1,0:T(8,128)(2,1)S(1)}, u32[]{:S(2)}, u32[]{:S(2)}) %collective-permute-start.10) | collective-permute-done | bytes 262176 | tf_op jit(solution)/shard_map/ppermute | solution.py:36
  45.2 7.6 %collective-permute-done.5.refs_2_ = bf16[2,128,1024]{2,1,0:T(8,128)(2,1)S(1)} collective-permute-done((bf16[2,128,1024]{2,1,0:T(8,128)(2,1)S(1)}, bf16[2,128,1024]{2,1,0:T(8,128)(2,1)S(1)}, u32[]{:S(2)}, u32[]{:S(2)}) %collective-permute-start.5) | collective-permute-done | bytes 524320 | tf_op jit(solution)/shard_map/ppermute | solution.py:36
  60.5 4.2 %collective-permute-done.8 = bf16[2,2,48,1024]{3,2,1,0:T(8,128)(2,1)S(1)} collective-permute-done((bf16[2,2,48,1024]{3,2,1,0:T(8,128)(2,1)S(1)}, bf16[2,2,48,1024]{3,2,1,0:T(8,128)(2,1)S(1)}, u32[]{:S(2)}, u32[]{:S(2)}) %collective-permute-start.8) | collective-permute-done | bytes 393248 | tf_op jit(solution)/shard_map/ppermute | solution.py:36
  66.6 3.1 %collective-permute-done.6.refs_1_ = bf16[2,2,48,1024]{3,2,1,0:T(8,128)(2,1)S(1)} collective-permute-done((bf16[2,2,48,1024]{3,2,1,0:T(8,128)(2,1)S(1)}, bf16[2,2,48,1024]{3,2,1,0:T(8,128)(2,1)S(1)}, u32[]{:S(2)}, u32[]{:S(2)}) %collective-permute-start.6) | collective-permute-done | bytes 393248 | tf_op jit(solution)/shard_map/ppermute | solution.py:36
  74.9 4.2 %multiply_convert_fusion.2 = (bf16[768,768]{1,0:T(8,128)(2,1)S(1)}, f32[768,768]{1,0:T(8,128)}) fusion(f32[768,768]{1,0:T(8,128)S(1)} %fusion.57, bf16[768,2048]{1,0:T(8,128)(2,1)S(1)} %bitcast.172, bf16[768,2048]{1,0:T(8,128)(2,1)S(1)} %copy-done.3), kind=kOutput, calls=%fused_computation.5 | convolution fusion | flops 2419458048 | bytes 12189696 | tf_op jit(solution)/shard_map/dot_general | solution.py:512
  79.0 5.1 %row_sums.1 = (f32[4,4,4,128]{3,2,1,0:T(4,128)S(1)}, f32[4,4,48,128]{3,2,1,0:T(8,128)S(1)}) custom-call(bf16[4,4,48,768]{3,2,1,0:T(8,128)(2,1)S(1)} %bitcast.177, bf16[768,128]{1,0:T(8,128)(2,1)S(1)} %fusion.14.head_ref, f32[4,4,1,128]{3,2,1,0:T(1,128)S(1)} %bitcast.181, bf16[4,4,16,128]{3,2,1,0:T(8,128)(2,1)S(1)} %maximum_maximum_fusion.weight_ref), custom_call_target="tpu_custom_call" | custom-call | flops 150994944 | bytes 1572864 | tf_op jit(solution)/shard_map/row_sums/pallas_call | solution.py:297
  90.5 5.1 %out_rows.1.refs_1_ = bf16[2,2,2,4,48,1024]{5,4,3,2,1,0:T(8,128)(2,1)S(1)} custom-call(s32[2]{0:T(128)S(1)} %pad_add_fusion.place_ref, bf16[4,4,48,768]{3,2,1,0:T(8,128)(2,1)S(1)} %bitcast.178, bf16[768,2048]{1,0:T(8,128)(2,1)S(1)} %copy-done, f32[4,4,48,128]{3,2,1,0:T(8,128)S(1)} %get-tuple-element.38.refs_2_), custom_call_target="tpu_custom_call" | custom-call | flops 2415919104 | bytes 7471104 | tf_op jit(solution)/shard_map/out_rows/pallas_call | solution.py:244
  95.7 3.1 %collective-permute-start.22 = (f32[4,2,2,4,128]{4,3,2,1,0:T(4,128)S(1)}, f32[4,2,2,4,128]{4,3,2,1,0:T(4,128)S(1)}, u32[]{:S(2)}, u32[]{:S(2)}) collective-permute-start(f32[4,2,2,4,128]{4,3,2,1,0:T(4,128)S(1)} %add.103), channel_id=1, source_target_pairs={{0,16},{1,17},{2,18},{3,19},{4,20},{5,21},{6,22},{7,23},{8,24},{9,... | collective-permute-start | bytes 98312 | tf_op jit(solution)/shard_map/ppermute | solution.py:36
  105.5 8.0 %collective-permute-done.36.refs_1_ = bf16[2,4,48,1024]{3,2,1,0:T(8,128)(2,1)S(1)} collective-permute-done((bf16[2,4,48,1024]{3,2,1,0:T(8,128)(2,1)S(1)}, bf16[2,4,48,1024]{3,2,1,0:T(8,128)(2,1)S(1)}, u32[]{:S(2)}, u32[]{:S(2)}) %collective-permute-start.36) | collective-permute-done | bytes 786464 | tf_op jit(solution)/shard_map/ppermute | solution.py:36
  113.6 5.3 %gradient_rows.1 = bf16[4,4,48,2048]{3,2,1,0:T(8,128)(2,1)S(1)} custom-call(s32[2]{0:T(128)S(1)} %pad_add_fusion.place_ref, bf16[2,4,48,1024]{3,2,1,0:T(8,128)(2,1)S(1)} %get-tuple-element.42.refs_0_, bf16[2,4,48,1024]{3,2,1,0:T(8,128)(2,1)S(1)} %collective-permute-done.36.refs_1_, bf16[2,4,48,1024]{3,2,1,0:T(8,128)(2,1)S(1)} %collective-permute-done.37.refs_2_, ...), custom_call_target="tpu_custom_call" | custom-call | flops 15728640 | bytes 6291456 | tf_op jit(solution)/shard_map/gradient_rows/pallas_call | solution.py:193
  118.9 4.8 %multiply_convert_fusion = (bf16[768,768]{1,0:T(8,128)(2,1)S(1)}, bf16[768,768]{1,0:T(8,128)(2,1)S(1)}) fusion(f32[768,768]{1,0:T(8,128)S(1)} %copy-done.9, f32[768,768]{1,0:T(8,128)} %get-tuple-element.87, bf16[768,2048]{1,0:T(8,128)(2,1)S(1)} %bitcast.175, bf16[768,2048]{1,0:T(8,128)(2,1)S(1)} %copy-done), kind=kOutput, calls=%fused_computation.3 | convolution fusion | flops 2423586816 | bytes 13369344 | tf_op jit(solution)/shard_map/dot_general | solution.py:512
  123.7 7.8 %d_rows.1 = (bf16[2,2,2,2,48,1024]{5,4,3,2,1,0:T(8,128)(2,1)S(1)}, bf16[2,2,2,2,48,1024]{5,4,3,2,1,0:T(8,128)(2,1)S(1)}) custom-call(s32[2]{0:T(128)S(1)} %pad_add_fusion.place_ref, bf16[4,4,48,768]{3,2,1,0:T(8,128)(2,1)S(1)} %bitcast.183, bf16[768,2048]{1,0:T(8,128)(2,1)S(1)} %copy-done.2, bf16[4,4,48,768]{3,2,1,0:T(8,128)(2,1)S(1)} %bitcast.184, ...), custom_call_target="tpu_custom_call" | custom-call | flops 4831838208 | bytes 11796480 | tf_op jit(solution)/shard_map/d_rows/pallas_call | solution.py:244
  138.8 5.7 %collective-permute-done.26.refs_4_ = bf16[2,4,48,1024]{3,2,1,0:T(8,128)(2,1)S(1)} collective-permute-done((bf16[2,4,48,1024]{3,2,1,0:T(8,128)(2,1)S(1)}, bf16[2,4,48,1024]{3,2,1,0:T(8,128)(2,1)S(1)}, u32[]{:S(2)}, u32[]{:S(2)}) %collective-permute-start.26) | collective-permute-done | bytes 786464 | tf_op jit(solution)/shard_map/ppermute | solution.py:36
  149.4 16.9 %collective-permute-done.46.refs_4_ = bf16[2,2,48,1024]{3,2,1,0:T(8,128)(2,1)S(1)} collective-permute-done((bf16[2,2,48,1024]{3,2,1,0:T(8,128)(2,1)S(1)}, bf16[2,2,48,1024]{3,2,1,0:T(8,128)(2,1)S(1)}, u32[]{:S(2)}, u32[]{:S(2)}) %collective-permute-start.46) | collective-permute-done | bytes 393248 | tf_op jit(solution)/shard_map/ppermute | solution.py:36
  168.6 6.0 %collective-permute-done.42.refs_4_ = bf16[2,2,48,1024]{3,2,1,0:T(8,128)(2,1)S(1)} collective-permute-done((bf16[2,2,48,1024]{3,2,1,0:T(8,128)(2,1)S(1)}, bf16[2,2,48,1024]{3,2,1,0:T(8,128)(2,1)S(1)}, u32[]{:S(2)}, u32[]{:S(2)}) %collective-permute-start.42) | collective-permute-done | bytes 393248 | tf_op jit(solution)/shard_map/ppermute | solution.py:36
  177.1 4.0 %convolution_convert_fusion = bf16[768,2048]{1,0:T(8,128)(2,1)} fusion(bf16[768,768]{1,0:T(8,128)(2,1)S(1)} %get-tuple-element.86, bf16[768,2048]{1,0:T(8,128)(2,1)S(1)} %bitcast.176), kind=kOutput, calls=%fused_computation | convolution fusion | flops 2417491968 | bytes 7471104 | tf_op jit(solution)/shard_map/dot_general | solution.py:515
  192.4 11.6 %collective-permute-start.29 = (bf16[128,1024]{1,0:T(8,128)(2,1)S(1)}, bf16[128,1024]{1,0:T(8,128)(2,1)S(1)}, u32[]{:S(2)}, u32[]{:S(2)}) collective-permute-start(bf16[128,1024]{1,0:T(8,128)(2,1)S(1)} %get-tuple-element.72), channel_id=1, source_target_pairs={{0,16},{1,17},{2,18},{3,19},{4,20},{5,21},{6,22},{7,23},{8,24},{9,... | collective-permute-start | bytes 786440 | tf_op jit(solution)/shard_map/ppermute | solution.py:36
  204.0 4.0 %convolution_convert_fusion.1 = bf16[768,2048]{1,0:T(8,128)(2,1)} fusion(bf16[768,768]{1,0:T(8,128)(2,1)S(1)} %get-tuple-element.66, bf16[768,2048]{1,0:T(8,128)(2,1)S(1)} %bitcast.173), kind=kOutput, calls=%fused_computation.1 | convolution fusion | flops 2417491968 | bytes 7471104 | tf_op jit(solution)/shard_map/dot_general | solution.py:515
  208.0 5.7 %collective-permute-done.49 = bf16[128,1024]{1,0:T(8,128)(2,1)S(1)} collective-permute-done((bf16[128,1024]{1,0:T(8,128)(2,1)S(1)}, bf16[128,1024]{1,0:T(8,128)(2,1)S(1)}, u32[]{:S(2)}, u32[]{:S(2)}) %collective-permute-start.49) | collective-permute-done | bytes 262176 | tf_op jit(solution)/shard_map/ppermute | solution.py:36
  213.8 13.3 %collective-permute-done.29 = bf16[128,1024]{1,0:T(8,128)(2,1)S(1)} collective-permute-done((bf16[128,1024]{1,0:T(8,128)(2,1)S(1)}, bf16[128,1024]{1,0:T(8,128)(2,1)S(1)}, u32[]{:S(2)}, u32[]{:S(2)}) %collective-permute-start.29) | collective-permute-done | bytes 262176 | tf_op jit(solution)/shard_map/ppermute | solution.py:36
  229.5 4.0 %convolution_convert_fusion.2 = bf16[768,2048]{1,0:T(8,128)(2,1)} fusion(bf16[768,768]{1,0:T(8,128)(2,1)S(1)} %get-tuple-element.67, bf16[768,2048]{1,0:T(8,128)(2,1)S(1)} %bitcast.174), kind=kOutput, calls=%fused_computation.2 | convolution fusion | flops 2417491968 | bytes 7471104 | tf_op jit(solution)/shard_map/dot_general | solution.py:515
  (202 shorter events, 86.4 us)
Async XLA Ops:
  8.4 14.7 %collective-permute-start.11 = (bf16[128,1024]{1,0:T(8,128)(2,1)}, bf16[128,1024]{1,0:T(8,128)(2,1)S(1)}, u32[]{:S(2)}, u32[]{:S(2)}) collective-permute-start(bf16[128,1024]{1,0:T(8,128)(2,1)} %param.10), channel_id=1, source_target_pairs={{0,24},{1,25},{2,26},{3,27},{4,28},{5,29},{6,30},{7,31},{8,16},{9,... | collective-permute-start | bytes 786440 | tf_op jit(solution)/shard_map/ppermute | solution.py:36
  12.3 21.2 %collective-permute-start.10 = (bf16[128,1024]{1,0:T(8,128)(2,1)}, bf16[128,1024]{1,0:T(8,128)(2,1)S(1)}, u32[]{:S(2)}, u32[]{:S(2)}) collective-permute-start(bf16[128,1024]{1,0:T(8,128)(2,1)} %param.10), channel_id=1, source_target_pairs={{0,16},{1,17},{2,18},{3,19},{4,20},{5,21},{6,22},{7,23},{8,24},{9,... | collective-permute-start | bytes 786440 | tf_op jit(solution)/shard_map/ppermute | solution.py:36
  15.2 19.8 %collective-permute-start.4 = (bf16[128,1024]{1,0:T(8,128)(2,1)}, bf16[128,1024]{1,0:T(8,128)(2,1)S(1)}, u32[]{:S(2)}, u32[]{:S(2)}) collective-permute-start(bf16[128,1024]{1,0:T(8,128)(2,1)} %param.10), channel_id=1, source_target_pairs={{0,8},{1,9},{2,10},{3,11},{4,12},{5,13},{6,14},{7,15},{8,0},{9,1},... | collective-permute-start | bytes 786440 | tf_op jit(solution)/shard_map/ppermute | solution.py:36
  23.0 12.9 %collective-permute-start.18 = (f32[4,2,24,128]{3,2,0,1:T(8,128)S(1)}, f32[4,2,24,128]{3,2,0,1:T(8,128)S(1)}, u32[]{:S(2)}, u32[]{:S(2)}) collective-permute-start(f32[4,2,24,128]{3,2,0,1:T(8,128)S(1)} %get-tuple-element.76), channel_id=1, source_target_pairs={{0,2},{1,3},{2,0},{3,1},{4,6},{5,7},{6,4},{7,5},{8,10},{9,11},{10,... | collective-permute-start | bytes 294920 | tf_op jit(solution)/shard_map/ppermute | solution.py:36
  35.1 17.6 %collective-permute-start.5 = (bf16[2,128,1024]{2,1,0:T(8,128)(2,1)S(1)}, bf16[2,128,1024]{2,1,0:T(8,128)(2,1)S(1)}, u32[]{:S(2)}, u32[]{:S(2)}) collective-permute-start(bf16[2,128,1024]{2,1,0:T(8,128)(2,1)S(1)} %pad_maximum_fusion.1.refs_1_), channel_id=1, source_target_pairs={{0,4},{1,5},{2,3},{3,2},{4,0},{5,1},{6,7},{7,6},{8,12},{9,13},{10,... | collective-permute-start | bytes 1572872 | tf_op jit(solution)/shard_map/ppermute | solution.py:36
  36.0 19.1 %collective-permute-start.34 = (bf16[128,1024]{1,0:T(8,128)(2,1)S(1)}, bf16[128,1024]{1,0:T(8,128)(2,1)S(1)}, u32[]{:S(2)}, u32[]{:S(2)}) collective-permute-start(bf16[128,1024]{1,0:T(8,128)(2,1)S(1)} %copy-done.5), channel_id=1, source_target_pairs={{0,24},{1,25},{2,26},{3,27},{4,28},{5,29},{6,30},{7,31},{8,16},{9,... | collective-permute-start | bytes 786440 | tf_op jit(solution)/shard_map/ppermute | solution.py:36
  38.4 19.7 %collective-permute-start.33 = (bf16[128,1024]{1,0:T(8,128)(2,1)S(1)}, bf16[128,1024]{1,0:T(8,128)(2,1)S(1)}, u32[]{:S(2)}, u32[]{:S(2)}) collective-permute-start(bf16[128,1024]{1,0:T(8,128)(2,1)S(1)} %copy-done.5), channel_id=1, source_target_pairs={{0,16},{1,17},{2,18},{3,19},{4,20},{5,21},{6,22},{7,23},{8,24},{9,... | collective-permute-start | bytes 786440 | tf_op jit(solution)/shard_map/ppermute | solution.py:36
  38.4 19.7 %collective-permute-start.32 = (bf16[128,1024]{1,0:T(8,128)(2,1)S(1)}, bf16[128,1024]{1,0:T(8,128)(2,1)S(1)}, u32[]{:S(2)}, u32[]{:S(2)}) collective-permute-start(bf16[128,1024]{1,0:T(8,128)(2,1)S(1)} %copy-done.5), channel_id=1, source_target_pairs={{0,8},{1,9},{2,10},{3,11},{4,12},{5,13},{6,14},{7,15},{8,0},{9,1},... | collective-permute-start | bytes 786440 | tf_op jit(solution)/shard_map/ppermute | solution.py:36
  43.6 16.0 %collective-permute-start.13 = (bf16[2,2,48,1024]{3,2,1,0:T(8,128)(2,1)S(1)}, bf16[2,2,48,1024]{3,2,1,0:T(8,128)(2,1)S(1)}, u32[]{:S(2)}, u32[]{:S(2)}) collective-permute-start(bf16[2,2,48,1024]{3,2,1,0:T(8,128)(2,1)S(1)} %get-tuple-element.34), channel_id=1, source_target_pairs={{0,1},{1,0},{2,6},{3,7},{4,5},{5,4},{6,2},{7,3},{8,9},{9,8},{10,14... | collective-permute-start | bytes 1179656 | tf_op jit(solution)/shard_map/ppermute | solution.py:36
  65.0 22.1 %collective-permute-start.35 = (bf16[4,128,1024]{2,1,0:T(8,128)(2,1)S(1)}, bf16[4,128,1024]{2,1,0:T(8,128)(2,1)S(1)}, u32[]{:S(2)}, u32[]{:S(2)}) collective-permute-start(bf16[4,128,1024]{2,1,0:T(8,128)(2,1)S(1)} %pad_maximum_fusion.refs_1_), channel_id=1, source_target_pairs={{0,4},{1,5},{2,3},{3,2},{4,0},{5,1},{6,7},{7,6},{8,12},{9,13},{10,... | collective-permute-start | bytes 3145736 | tf_op jit(solution)/shard_map/ppermute | solution.py:36
  88.8 16.0 %collective-permute-start.38 = (bf16[2,4,48,1024]{3,2,1,0:T(8,128)(2,1)S(1)}, bf16[2,4,48,1024]{3,2,1,0:T(8,128)(2,1)S(1)}, u32[]{:S(2)}, u32[]{:S(2)}) collective-permute-start(bf16[2,4,48,1024]{3,2,1,0:T(8,128)(2,1)S(1)} %get-tuple-element.45), channel_id=1, source_target_pairs={{0,1},{1,0},{2,6},{3,7},{4,5},{5,4},{6,2},{7,3},{8,9},{9,8},{10,14... | collective-permute-start | bytes 2359304 | tf_op jit(solution)/shard_map/ppermute | solution.py:36
  103.0 33.8 %collective-permute-start.25 = (bf16[2,4,48,1024]{3,2,1,0:T(8,128)(2,1)S(1)}, bf16[2,4,48,1024]{3,2,1,0:T(8,128)(2,1)S(1)}, u32[]{:S(2)}, u32[]{:S(2)}) collective-permute-start(bf16[2,4,48,1024]{3,2,1,0:T(8,128)(2,1)S(1)} %slice_bitcast_fusion.2), channel_id=1, source_target_pairs={{0,1},{1,0},{2,6},{3,7},{4,5},{5,4},{6,2},{7,3},{8,9},{9,8},{10,14... | collective-permute-start | bytes 2359304 | tf_op jit(solution)/shard_map/ppermute | solution.py:36
  104.7 27.6 %collective-permute-start.24 = (bf16[2,2,4,48,1024]{4,3,2,1,0:T(8,128)(2,1)S(1)}, bf16[2,2,4,48,1024]{4,3,2,1,0:T(8,128)(2,1)S(1)}, u32[]{:S(2)}, u32[]{:S(2)}) collective-permute-start(bf16[2,2,4,48,1024]{4,3,2,1,0:T(8,128)(2,1)S(1)} %slice_bitcast_fusion), channel_id=1, source_target_pairs={{0,2},{1,3},{2,0},{3,1},{4,6},{5,7},{6,4},{7,5},{8,10},{9,11},{10,... | collective-permute-start | bytes 4718600 | tf_op jit(solution)/shard_map/ppermute | solution.py:36
  133.9 15.5 %collective-permute-start.45 = (bf16[2,2,48,1024]{3,2,1,0:T(8,128)(2,1)S(1)}, bf16[2,2,48,1024]{3,2,1,0:T(8,128)(2,1)S(1)}, u32[]{:S(2)}, u32[]{:S(2)}) collective-permute-start(bf16[2,2,48,1024]{3,2,1,0:T(8,128)(2,1)S(1)} %slice_bitcast_fusion.9), channel_id=1, source_target_pairs={{0,1},{1,0},{2,6},{3,7},{4,5},{5,4},{6,2},{7,3},{8,9},{9,8},{10,14... | collective-permute-start | bytes 1179656 | tf_op jit(solution)/shard_map/ppermute | solution.py:36
  134.6 34.1 %collective-permute-start.41 = (bf16[2,2,48,1024]{3,2,1,0:T(8,128)(2,1)S(1)}, bf16[2,2,48,1024]{3,2,1,0:T(8,128)(2,1)S(1)}, u32[]{:S(2)}, u32[]{:S(2)}) collective-permute-start(bf16[2,2,48,1024]{3,2,1,0:T(8,128)(2,1)S(1)} %slice_bitcast_fusion.10), channel_id=1, source_target_pairs={{0,1},{1,0},{2,6},{3,7},{4,5},{5,4},{6,2},{7,3},{8,9},{9,8},{10,14... | collective-permute-start | bytes 1179656 | tf_op jit(solution)/shard_map/ppermute | solution.py:36
  136.0 30.2 %collective-permute-start.46 = (bf16[2,2,48,1024]{3,2,1,0:T(8,128)(2,1)S(1)}, bf16[2,2,48,1024]{3,2,1,0:T(8,128)(2,1)S(1)}, u32[]{:S(2)}, u32[]{:S(2)}) collective-permute-start(bf16[2,2,48,1024]{3,2,1,0:T(8,128)(2,1)S(1)} %slice_bitcast_fusion.7), channel_id=1, source_target_pairs={{0,1},{1,0},{2,6},{3,7},{4,5},{5,4},{6,2},{7,3},{8,9},{9,8},{10,14... | collective-permute-start | bytes 1179656 | tf_op jit(solution)/shard_map/ppermute | solution.py:36
  136.8 37.9 %collective-permute-start.42 = (bf16[2,2,48,1024]{3,2,1,0:T(8,128)(2,1)S(1)}, bf16[2,2,48,1024]{3,2,1,0:T(8,128)(2,1)S(1)}, u32[]{:S(2)}, u32[]{:S(2)}) collective-permute-start(bf16[2,2,48,1024]{3,2,1,0:T(8,128)(2,1)S(1)} %slice_bitcast_fusion.8), channel_id=1, source_target_pairs={{0,1},{1,0},{2,6},{3,7},{4,5},{5,4},{6,2},{7,3},{8,9},{9,8},{10,14... | collective-permute-start | bytes 1179656 | tf_op jit(solution)/shard_map/ppermute | solution.py:36
  146.1 40.7 %collective-permute-start.27 = (bf16[4,128,1024]{2,1,0:T(8,128)(2,1)S(1)}, bf16[4,128,1024]{2,1,0:T(8,128)(2,1)S(1)}, u32[]{:S(2)}, u32[]{:S(2)}) collective-permute-start(bf16[4,128,1024]{2,1,0:T(8,128)(2,1)S(1)} %get-tuple-element.40), channel_id=1, source_target_pairs={{0,4},{1,5},{2,3},{3,2},{4,0},{5,1},{6,7},{7,6},{8,12},{9,13},{10,... | collective-permute-start | bytes 3145736 | tf_op jit(solution)/shard_map/ppermute | solution.py:36
  167.1 14.0 %collective-permute-start.47 = (bf16[2,128,1024]{2,1,0:T(8,128)(2,1)S(1)}, bf16[2,128,1024]{2,1,0:T(8,128)(2,1)S(1)}, u32[]{:S(2)}, u32[]{:S(2)}) collective-permute-start(bf16[2,128,1024]{2,1,0:T(8,128)(2,1)S(1)} %get-tuple-element.51), channel_id=1, source_target_pairs={{0,4},{1,5},{2,3},{3,2},{4,0},{5,1},{6,7},{7,6},{8,12},{9,13},{10,... | collective-permute-start | bytes 1572872 | tf_op jit(solution)/shard_map/ppermute | solution.py:36
  183.8 30.0 %collective-permute-start.49 = (bf16[128,1024]{1,0:T(8,128)(2,1)S(1)}, bf16[128,1024]{1,0:T(8,128)(2,1)S(1)}, u32[]{:S(2)}, u32[]{:S(2)}) collective-permute-start(bf16[128,1024]{1,0:T(8,128)(2,1)S(1)} %get-tuple-element.74), channel_id=1, source_target_pairs={{0,16},{1,17},{2,18},{3,19},{4,20},{5,21},{6,22},{7,23},{8,24},{9,... | collective-permute-start | bytes 786440 | tf_op jit(solution)/shard_map/ppermute | solution.py:36
  185.0 28.8 %collective-permute-start.50 = (bf16[128,1024]{1,0:T(8,128)(2,1)S(1)}, bf16[128,1024]{1,0:T(8,128)(2,1)S(1)}, u32[]{:S(2)}, u32[]{:S(2)}) collective-permute-start(bf16[128,1024]{1,0:T(8,128)(2,1)S(1)} %fusion.15), channel_id=1, source_target_pairs={{0,8},{1,9},{2,10},{3,11},{4,12},{5,13},{6,14},{7,15},{8,0},{9,1},... | collective-permute-start | bytes 786440 | tf_op jit(solution)/shard_map/ppermute | solution.py:36
  187.4 26.4 %collective-permute-start.28 = (bf16[128,1024]{1,0:T(8,128)(2,1)S(1)}, bf16[128,1024]{1,0:T(8,128)(2,1)S(1)}, u32[]{:S(2)}, u32[]{:S(2)}) collective-permute-start(bf16[128,1024]{1,0:T(8,128)(2,1)S(1)} %get-tuple-element.70), channel_id=1, source_target_pairs={{0,24},{1,25},{2,26},{3,27},{4,28},{5,29},{6,30},{7,31},{8,16},{9,... | collective-permute-start | bytes 786440 | tf_op jit(solution)/shard_map/ppermute | solution.py:36
  190.0 23.8 %collective-permute-start.30 = (bf16[128,1024]{1,0:T(8,128)(2,1)S(1)}, bf16[128,1024]{1,0:T(8,128)(2,1)S(1)}, u32[]{:S(2)}, u32[]{:S(2)}) collective-permute-start(bf16[128,1024]{1,0:T(8,128)(2,1)S(1)} %get-tuple-element.71), channel_id=1, source_target_pairs={{0,8},{1,9},{2,10},{3,11},{4,12},{5,13},{6,14},{7,15},{8,0},{9,1},... | collective-permute-start | bytes 786440 | tf_op jit(solution)/shard_map/ppermute | solution.py:36
  192.4 34.7 %collective-permute-start.29 = (bf16[128,1024]{1,0:T(8,128)(2,1)S(1)}, bf16[128,1024]{1,0:T(8,128)(2,1)S(1)}, u32[]{:S(2)}, u32[]{:S(2)}) collective-permute-start(bf16[128,1024]{1,0:T(8,128)(2,1)S(1)} %get-tuple-element.72), channel_id=1, source_target_pairs={{0,16},{1,17},{2,18},{3,19},{4,20},{5,21},{6,22},{7,23},{8,24},{9,... | collective-permute-start | bytes 786440 | tf_op jit(solution)/shard_map/ppermute | solution.py:36
  (39 other events, 337.2 us)
where the time goes:
time: 239 us; the launch traced here: 238 us
  waiting for transfers between devices  97.8 us (41%)
  starting transfers between devices  69.2 us (29%)
  Pallas kernels  32.5 us (14%)
  matrix products  29.3 us (12%)
  other arithmetic  6.97 us (3%)
    ppermute x52, waiting for transfers between devices, send(): return lax.ppermute(value, ('ep', 'tp'), pairs)  97.8 us
    ppermute x52, starting transfers between devices, send(): return lax.ppermute(value, ('ep', 'tp'), pairs)  69.2 us
    pallas_call x2, Pallas kernels, column_product(): pl.pallas_call(body, grid_spec=pltpu.PrefetchScalarGridSpec(num_scalar_pr...  13 us
    dot_general x3, matrix products, over_rows(): lax.dot_general(left, right, (((0,), (0,)), ((), ())), preferred_element_...  12 us
    dot_general x3, matrix products, against(): lax.dot_general(left, right, (((1,), (1,)), ((), ())), preferred_element_...  11.6 us
    pallas_call x2, Pallas kernels, assemble(): pl.pallas_call(body, grid_spec=pltpu.PrefetchScalarGridSpec(num_scalar_pr...  7.79 us
    pallas_call x1, Pallas kernels, row_sums(): pl.pallas_call(body, grid=(depth,), in_specs=[pl.BlockSpec((1, 2 * n, cap...  5.05 us
  transfers between devices with their start and end apart: 52, of which 21 were waited for; matrix products, arithmetic and copies ran while one was open for 14% of the time, Pallas kernels for 14%

commit v1 on v0

--- a/solution.py
+++ b/solution.py
@@ -58,6 +58,27 @@
 
 def send_last(value, k):
     return send(value, lambda i, j: (i ^ (2 * k), j) if i % 2 else (i, j ^ k))
+
+
+def z_gather(value, depth, n):
+    column = {0: value}
+    bit = depth // 2
+    while bit:
+        for k in list(column):
+            column[k ^ bit] = send_z(column[k], bit, n)
+        bit //= 2
+    return [column[k] for k in range(depth)]
+
+
+def z_reduce(column, n):
+    blocks = dict(enumerate(column))
+    bit = 1
+    while bit < len(column):
+        for k in sorted(blocks, reverse=True):
+            if k & bit:
+                blocks[k ^ bit] = blocks[k ^ bit] + send_z(blocks.pop(k).astype(BF), bit, n).astype(F32)
+        bit *= 2
+    return blocks[0]
 
 
 def xor_blocks(value, axis, index):
@@ -81,33 +102,36 @@
     return pl.BlockSpec(shape, lambda *_: (0,) * len(shape))
 
 
-def selector(pos_ref, h, cap, experts, tokens):
+def selector(pos_ref, h, z, cap, experts, tokens):
     slots = lax.broadcasted_iota(jnp.int32, (cap, tokens), 0).astype(F32)
     parts = [
-        jnp.where(pos_ref[h, 0, e : e + 1, :] == slots, 1.0, 0.0).astype(F32) for e in range(experts)
+        jnp.where(pos_ref[h, z, e : e + 1, :] == slots, 1.0, 0.0).astype(F32) for e in range(experts)
     ]
     return jnp.concatenate(parts, axis=0).astype(BF)
 
 
-def pick_rows(units, pos, start, cap):
-    n = len(units)
-    group, tokens, width = units[0].shape
-    experts = pos.shape[2]
-
-    def body(*refs):
-        pos_ref, ins, outs = refs[0], refs[1 : 1 + n], refs[1 + n :]
-        for h in range(n):
-            chosen = selector(pos_ref, h, cap, experts, tokens)
-            rows = jnp.dot(chosen, ins[h][0], preferred_element_type=F32).astype(BF)
-            for e in range(experts):
-                outs[e][h, 0] = rows[e * cap : (e + 1) * cap]
-
+def pick_rows(units, after, pos, start, cap):
+    n, _, experts, tokens = pos.shape
+    stacked = not isinstance(units[0], (list, tuple))
+    group = units[0].shape[0] if stacked else len(units)
+    flat = list(units) if stacked else [unit for at_z in units for unit in at_z]
+    width = flat[0].shape[-1]
+
+    def body(pos_ref, *refs):
+        ins, outs = refs[: len(flat)], refs[-experts:]
+        for z in range(group):
+            for h in range(n):
+                chosen = selector(pos_ref, h, start + z, cap, experts, tokens)
+                unit = ins[h][z] if stacked else ins[z * n + h][...]
+                rows = jnp.dot(chosen, unit, preferred_element_type=F32).astype(BF)
+                for e in range(experts):
+                    outs[e][h, z] = rows[e * cap : (e + 1) * cap]
+
+    vmem = pl.BlockSpec(memory_space=pltpu.VMEM)
     return pl.pallas_call(
         body,
-        grid=(group,),
-        in_specs=[pl.BlockSpec((n, 1, experts, tokens), lambda z: (0, z + start, 0, 0))]
-        + [pl.BlockSpec((1, tokens, width), lambda z: (z, 0, 0))] * n,
-        out_specs=[pl.BlockSpec((n, 1, cap, width), lambda z: (0, z, 0, 0))] * experts,
+        in_specs=[vmem] * (1 + len(flat)) + [pl.BlockSpec(memory_space=pl.ANY)] * len(after),
+        out_specs=[vmem] * experts,
         out_shape=[jax.ShapeDtypeStruct((n, group, cap, width), BF)] * experts,
         compiler_params=params(),
         cost_estimate=pl.CostEstimate(
@@ -116,16 +140,16 @@
             transcendentals=0,
         ),
         name="pick_rows",
-    )(pos, *units)
-
-
-def spread_rows(sources, pos, start, group, cap, width):
+    )(pos, *flat, *after)
+
+
+def spread_rows(sources, after, pos, start, group, cap, width):
     n, _, experts, tokens = pos.shape
 
     def body(*refs):
-        pos_ref, ins, outs = refs[0], refs[1 : 1 + experts], refs[1 + experts :]
+        pos_ref, ins, outs = refs[0], refs[1 : 1 + experts], refs[-n:]
         for h in range(n):
-            chosen = selector(pos_ref, h, cap, experts, tokens)
+            chosen = selector(pos_ref, h, 0, cap, experts, tokens)
             rows = jnp.concatenate(
                 [ref[(0,) * len(prefix) + (h, 0)] for ref, (_, prefix) in zip(ins, sources)], axis=0
             )
@@ -139,7 +163,8 @@
         body,
         grid=(group,),
         in_specs=[pl.BlockSpec((n, 1, experts, tokens), lambda z: (0, z + start, 0, 0))]
-        + [spec(prefix) for _, prefix in sources],
+        + [spec(prefix) for _, prefix in sources]
+        + [pl.BlockSpec(memory_space=pl.ANY)] * len(after),
         out_specs=[pl.BlockSpec((1, tokens, width), lambda z: (z, 0, 0))] * n,
         out_shape=[jax.ShapeDtypeStruct((group, tokens, width), BF)] * n,
         compiler_params=params(),
@@ -149,17 +174,17 @@
             transcendentals=0,
         ),
         name="spread_rows",
-    )(pos, *[array for array, _ in sources])
-
-
-def assemble(place, pieces, groups, finish, extra, extra_specs, model_width, name):
+    )(pos, *[array for array, _ in sources], *after)
+
+
+def assemble(place, pieces, groups, finish, extra, extra_specs, after, model_width, name):
     n = len(pieces[0][0])
     _, _, cap, width = pieces[0][0][0].shape
     depth = sum(len(g) for g in groups)
     count = len(groups) * 2 * n
 
     def body(place_ref, *refs):
-        ins, more, out_ref = refs[:count], refs[count:-1], refs[-1]
+        ins, more, out_ref = refs[:count], refs[count : count + len(extra)], refs[-1]
         z = pl.program_id(0)
         core, col = place_ref[0], place_ref[1]
 
@@ -179,8 +204,7 @@
                 fill(g)
             else:
                 pl.when(jnp.logical_and(z >= members[0], z <= members[-1]))(functools.partial(fill, g))
-        for b in range(2 * n):
-            out_ref[0, b] = finish(b, out_ref[0, b].astype(F32), *more)
+        finish(out_ref, *more)
 
     def piece_spec(members):
         first, last = members[0], members[-1]
@@ -195,7 +219,7 @@
         grid_spec=pltpu.PrefetchScalarGridSpec(
             num_scalar_prefetch=1,
             grid=(depth,),
-            in_specs=in_specs + extra_specs,
+            in_specs=in_specs + extra_specs + [pl.BlockSpec(memory_space=pl.ANY)] * len(after),
             out_specs=pl.BlockSpec((1, 2 * n, cap, model_width), lambda z, *_: (z, 0, 0, 0)),
         ),
         out_shape=jax.ShapeDtypeStruct((depth, 2 * n, cap, model_width), BF),
@@ -206,10 +230,10 @@
             transcendentals=0,
         ),
         name=name,
-    )(place, *flat, *extra)
-
-
-def column_product(place, terms, scale, groups, depth, n, cap, width, name):
+    )(place, *flat, *extra, *after)
+
+
+def column_product(place, terms, scale, after, groups, depth, n, cap, width, name):
     count = len(terms)
     units = terms[0][0].shape[1]
 
@@ -226,10 +250,17 @@
             term = jnp.dot(left, refs[2 * i + 1][...], preferred_element_type=F32)
             total = term if total is None else total + term
         rest = refs[2 * count :]
+        rows = total.reshape(depth, cap, width)
         if scale is not None:
-            total = total * rest[0][...].reshape(depth * cap, LANES)[:, :1]
-            rest = rest[1:]
-        rows = total.astype(BF).reshape(depth, cap, width)
+            rows = jnp.stack(
+                [
+                    rows[z] * row_weight(own_selector(rest[0][z, 0], cap), rest[1][z, 0])
+                    for z in range(depth)
+                ]
+            )
+            rest = rest[2:]
+        rows = rows.astype(BF)
+        rest = rest[len(after) :]
         for ref, members in zip(rest, groups):
             ref[0, 0, 0] = rows[members[0] : members[-1] + 1]
 
@@ -239,8 +270,12 @@
         in_specs += [left_spec, pl.BlockSpec((units, width), lambda y, b, *_: (0, y))]
         args += [left.reshape(depth, 2 * n, cap, units), right]
     if scale is not None:
-        in_specs.append(pl.BlockSpec((depth, 1, cap, LANES), lambda y, b, *_: (0, b, 0, 0)))
-        args.append(scale)
+        in_specs += [
+            pl.BlockSpec((depth, 1) + array.shape[2:], lambda y, b, *_: (0, b, 0, 0)) for array in scale
+        ]
+        args += scale
+    in_specs += [pl.BlockSpec(memory_space=pl.ANY)] * len(after)
+    args += after
     return pl.pallas_call(
         body,
         grid_spec=pltpu.PrefetchScalarGridSpec(
@@ -269,108 +304,125 @@
     )(place, *args)
 
 
-def own_selector(pos_ref, b, cap, tokens):
-    slots = lax.broadcasted_iota(jnp.int32, (cap, tokens), 0).astype(F32)
-    return jnp.where(pos_ref[0, b] == slots, 1.0, 0.0).astype(BF)
-
-
-def row_sums(active, down_head, pos_own, weight_parts, labels, depth, n, cap):
+def own_selector(pos, cap):
+    slots = lax.broadcasted_iota(jnp.int32, (cap, pos.shape[1]), 0).astype(F32)
+    return jnp.where(pos == slots, 1.0, 0.0).astype(BF)
+
+
+def wide_selector(pos_ref, blocks, cap):
+    tokens = pos_ref.shape[-1]
+    slots = lax.broadcasted_iota(jnp.int32, (blocks * cap, tokens), 0).astype(F32)
+    parts = []
+    for b in range(blocks):
+        pos = pos_ref[0, b]
+        parts.append(jnp.where(jnp.where(pos < 0, pos, pos + b * cap) == slots, 1.0, 0.0))
+    return jnp.concatenate(parts, axis=1).astype(BF)
+
+
+def row_weight(chosen, parts):
+    picked = lax.dot_general(chosen, parts, (((1,), (1,)), ((), ())), preferred_element_type=F32)
+    return picked[:, 0:1] + picked[:, 1:2] + picked[:, 2:3]
+
+
+def row_sums(active, down_head, pos_own, weight_own, after, labels, depth, n, cap):
     units = active.shape[1]
     tokens = pos_own.shape[-1]
 
-    def body(active_ref, head_ref, pos_ref, weight_ref, out_ref, scale_ref):
+    def body(active_ref, head_ref, pos_ref, weight_ref, *rest):
+        out_ref = rest[-1]
+        chosen = wide_selector(pos_ref, 2 * n, cap)
+        rows = active_ref[0].reshape(2 * n * cap, units)
+        sums = lax.dot_general(head_ref[...], rows, (((1,), (1,)), ((), ())), preferred_element_type=F32)
+        high = sums.astype(BF)
+        low = (sums - high.astype(F32)).astype(BF)
+        dense = jnp.dot(high, chosen, preferred_element_type=F32) + jnp.dot(
+            low, chosen, preferred_element_type=F32
+        )
         for b in range(2 * n):
-            chosen = own_selector(pos_ref, b, cap, tokens)
-            parts = lax.dot_general(
-                chosen, weight_ref[0, b], (((1,), (1,)), ((), ())), preferred_element_type=F32
-            )
-            scale = parts[:, 0:1] + parts[:, 1:2] + parts[:, 2:3]
-            scale_ref[0, b] = jnp.broadcast_to(scale, (cap, LANES))
-            rows = jnp.dot(active_ref[0, b], head_ref[...], preferred_element_type=F32) * scale
-            high = rows.astype(BF)
-            low = (rows - high.astype(F32)).astype(BF)
-            dense = lax.dot_general(
-                high, chosen, (((0,), (0,)), ((), ())), preferred_element_type=F32
-            ) + lax.dot_general(low, chosen, (((0,), (0,)), ((), ())), preferred_element_type=F32)
-            out_ref[0, b] = dense[0:labels] + dense[8 : 8 + labels]
+            own = dense[:, b * tokens : (b + 1) * tokens]
+            out_ref[0, b] = (own[0:labels] + own[8 : 8 + labels]) * weight_ref[0, b]
 
     return pl.pallas_call(
         body,
         grid=(depth,),
         in_specs=[
             pl.BlockSpec((1, 2 * n, cap, units), lambda z: (z, 0, 0, 0)),
-            whole_spec((units, LANES)),
+            whole_spec(down_head.shape),
             pl.BlockSpec((1, 2 * n, 1, tokens), lambda z: (z, 0, 0, 0)),
-            pl.BlockSpec((1, 2 * n, 16, tokens), lambda z: (z, 0, 0, 0)),
-        ],
-        out_specs=[
-            pl.BlockSpec((1, 2 * n, labels, tokens), lambda z: (z, 0, 0, 0)),
-            pl.BlockSpec((1, 2 * n, cap, LANES), lambda z: (z, 0, 0, 0)),
-        ],
-        out_shape=[
-            jax.ShapeDtypeStruct((depth, 2 * n, labels, tokens), F32),
-            jax.ShapeDtypeStruct((depth, 2 * n, cap, LANES), F32),
-        ],
+            pl.BlockSpec((1, 2 * n, 1, tokens), lambda z: (z, 0, 0, 0)),
+        ]
+        + [pl.BlockSpec(memory_space=pl.ANY)] * len(after),
+        out_specs=pl.BlockSpec((1, 2 * n, labels, tokens), lambda z: (z, 0, 0, 0)),
+        out_shape=jax.ShapeDtypeStruct((depth, 2 * n, labels, tokens), F32),
         compiler_params=params(),
         cost_estimate=pl.CostEstimate(
-            flops=2 * depth * 2 * n * cap * units * LANES,
-            bytes_accessed=2 * depth * 2 * n * cap * (units + 256),
+            flops=2 * depth * 2 * n * cap * units * 16,
+            bytes_accessed=2 * depth * 2 * n * cap * units,
             transcendentals=0,
         ),
         name="row_sums",
-    )(active.reshape(depth, 2 * n, cap, units), down_head, pos_own, weight_parts)
-
-
-def gather_rows(value, pos, groups, across, cap, column=None):
-    depth = sum(len(g) for g in groups)
-    n = across
-    if column is None:
-        column = [value] + [send_z(value, k, across) for k in range(1, depth)]
-    pieces = []
-    for members in groups:
-        stacked = jnp.stack([column[k] for k in members])
-        units = [stacked] + [send_first(stacked, k) for k in range(1, n)]
-        rows = pick_rows(units, pos, members[0], cap)
-        here, other = [], []
-        for f in range(n):
-            same, cross = rows[2 * f], rows[2 * f + 1]
-            if f > 0:
-                cross = send_last(cross, f)
-                same = send_last(same, f)
-            here.append(same)
-            other.append(send_core(cross))
-        pieces.append([here, other])
-    return pieces
-
-
-def return_rows(rows, pos, groups, across, cap):
-    n = across
-    width = rows[0].shape[-1]
-    column = {}
-    for g in reversed(range(len(groups))):
-        members = groups[g]
-        mine = rows[g]
-        crossed = send_core(mine[1])
-        sources = [(mine, (0, 0)), (crossed, (0,))]
-        for f in range(1, n):
-            sources += [(send_last(mine[0, f], f), ()), (send_last(crossed[f], f), ())]
-        dense = spread_rows(sources, pos, members[0], len(members), cap, width)
-        total = dense[0].astype(F32)
-        for h in range(1, n):
-            total = total + send_first(dense[h], h).astype(F32)
-        for i, k in enumerate(members):
-            column[k] = total[i]
-    result = column[0]
-    for k in sorted(column, reverse=True):
-        if k > 0:
-            result = result + send_z(column[k].astype(BF), k, across).astype(F32)
-    return result
-
-
-def sum_all(value):
+    )(active.reshape(depth, 2 * n, cap, units), down_head, pos_own, weight_own, *after)
+
+
+def route_rows(units, after, pos, start, cap):
+    rows = pick_rows(units, after, pos, start, cap)
+    n = pos.shape[0]
+    here, other = [], []
+    for f in range(n):
+        same, cross = rows[2 * f], rows[2 * f + 1]
+        if f > 0:
+            cross = send_last(cross, f)
+            same = send_last(same, f)
+        here.append(same)
+        other.append(send_core(cross))
+    return [here, other], rows
+
+
+def gather_by_column(column, after, pos, groups, n, cap):
+    units = [[value] + [send_first(value, k) for k in range(1, n)] for value in column]
+    routed = [
+        route_rows([units[k] for k in members], more, pos, members[0], cap)
+        for members, more in zip(groups, after)
+    ]
+    return [pieces for pieces, _ in routed], routed[0][1]
+
+
+def pick_at_once(column, pos, n, cap):
+    column = jnp.stack(column)
+    units = [column] + [send_first(column, k) for k in range(1, n)]
+    pieces, rows = route_rows(units, [], pos, 0, cap)
+    return [pieces], rows
+
+
+def return_sources(rows, crossed, n):
+    sources = [(rows, (0, 0)), (crossed, (0,))]
+    for f in range(1, n):
+        sources += [(send_last(rows[0, f], f), ()), (send_last(crossed[f], f), ())]
+    return sources
+
+
+def spread_back(rows, crossed, after, pos, start, n, cap):
+    group, _, width = rows.shape[3:]
+    return spread_rows(return_sources(rows, crossed, n), after, pos, start, group, cap, width)
+
+
+def first_sum(dense):
+    total = dense[0].astype(F32)
+    for h in range(1, len(dense)):
+        total = total + send_first(dense[h], h).astype(F32)
+    return total
+
+
+def sum_all(value, after, across, depth):
+    value = value + send_core(value)
     step = 1
-    while step < lax.axis_size("ep"):
-        value = value + send(value, lambda i, j: (i ^ step, j))
+    while step < depth:
+        value = value + send_z(value, step, across)
+        step *= 2
+    value = lax.optimization_barrier([value] + after)[0]
+    step = 1
+    while step < across:
+        value = value + send_x(value, step)
         step *= 2
     step = 1
     while step < lax.axis_size("tp"):
@@ -424,6 +476,8 @@
     def expert_of(ep_index, tp_index):
         return ep_index * local_count + tp_index * unit_rows // FF
 
+    hidden_column = z_gather(hidden_in, depth, n)
+
     spare = -(2 * top_count + 1) % 8
     meta = jnp.concatenate(
         [
@@ -433,22 +487,25 @@
             jnp.zeros((spare, tok_count), F32),
         ]
     )
-    meta = jnp.stack([meta] + [send_z(meta, k, across) for k in range(1, depth)])
+    meta = jnp.stack(z_gather(meta, depth, n))
     meta = jnp.stack([meta] + [send_x(meta, k) for k in range(1, n)], axis=1)
     meta = jnp.stack([meta, send_core(meta)], axis=1)
 
+    hidden_wide = hidden_in.astype(F32)
+    own_squares = jnp.sum(hidden_wide * hidden_wide, axis=1)
     feature_rows = jnp.concatenate(
         [
             norm_gain[None, :],
             head_weight.astype(F32).T,
-            jnp.zeros((-(1 + label_count) % 8, width), F32),
+            jnp.pad(own_squares[None, :], ((0, 0), (0, width - tok_count))),
+            jnp.zeros((-(2 + label_count) % 8, width), F32),
         ]
     )
     own_gain, own_head = feature_rows[0], feature_rows[1 : 1 + label_count]
     all_features = jnp.stack([feature_rows] + [send_y(feature_rows, j) for j in range(1, n)], axis=1)
+    squares = jnp.sum(all_features[1 + label_count, :, :tok_count], axis=0)
+    inv_rms = lax.rsqrt(squares / model_width + EPS)[:, None]
     all_features = xor_blocks(all_features, 1, col).reshape(feature_rows.shape[0], model_width)
-
-    hidden_column = [hidden_in] + [send_z(hidden_in, k, across) for k in range(1, depth)]
 
     spot = jnp.arange(tok_count, dtype=jnp.int32)
     earlier = (spot[:, None] < spot[None, :]).astype(BF)
@@ -477,36 +534,39 @@
     weight_parts = jnp.concatenate(split_bf(weight_own, 3) + [blank], axis=2)
     label_all = meta[..., 2 * top_count, :]
 
-    hidden_wide = hidden_in.astype(F32)
-    own_squares = jnp.sum(hidden_wide * hidden_wide, axis=1)
-    squares = own_squares
-    for j in range(1, n):
-        squares = squares + send_y(own_squares, j)
-    inv_rms = lax.rsqrt(squares / model_width + EPS)[:, None]
-
-    head_pair = jnp.concatenate([all_features[1:], jnp.zeros((1, model_width), F32)])
-    head_pad = jnp.concatenate(
-        [head_pair, head_pair, jnp.zeros((LANES - 16, model_width), F32)]
-    ).astype(BF)
+    head_pair = jnp.concatenate(
+        [all_features[1 : 1 + label_count], jnp.zeros((8 - label_count, model_width), F32)]
+    )
+    head_pair = jnp.concatenate([head_pair, head_pair]).astype(BF)
     down_head = lax.dot_general(
-        down_weight, head_pad, (((1,), (1,)), ((), ())), preferred_element_type=F32
+        head_pair, down_weight, (((1,), (1,)), ((), ())), preferred_element_type=F32
     )
     high = down_head.astype(BF)
-    lane = lax.broadcasted_iota(jnp.int32, down_head.shape, 1)
-    down_head = jnp.where(lane < 8, high, (down_head - high.astype(F32)).astype(BF))
-
-    pieces = gather_rows(hidden_in, pos, two, across, cap, hidden_column)
-
-    def normed(b, value, features_ref):
-        rms = lax.rsqrt(jnp.sum(value * value, axis=1, keepdims=True) / model_width + EPS)
-        return (value * rms * features_ref[0:1, :]).astype(BF)
+    which = lax.broadcasted_iota(jnp.int32, down_head.shape, 0)
+    down_head = jnp.where(which < 8, high, (down_head - high.astype(F32)).astype(BF))
+
+    later_in = lax.optimization_barrier([grad_later, hidden_column[depth // 2]])[0]
+    later_column = z_gather(later_in, depth, n)
+    pieces, _ = gather_by_column(hidden_column, [[], later_column[depth // 2 : depth // 2 + 1]], pos, two, n, cap)
+
+    def normed(out_ref, features_ref):
+        for b in range(2 * n):
+            value = out_ref[0, b].astype(F32)
+            rms = lax.rsqrt(jnp.sum(value * value, axis=1, keepdims=True) / model_width + EPS)
+            out_ref[0, b] = (value * rms * features_ref[0:1, :]).astype(BF)
 
     received = assemble(
-        place, pieces, two, normed, [all_features], [whole_spec(all_features.shape)], model_width, "normed_rows"
+        place,
+        pieces,
+        two,
+        normed,
+        [all_features],
+        [whole_spec(all_features.shape)],
+        [],
+        model_width,
+        "normed_rows",
     ).reshape(row_count, model_width)
-
-    later_in = lax.optimization_barrier([grad_later] + hidden_column)[0]
-    later = gather_rows(later_in, pos, one, across, cap)
+    later, picked_later = pick_at_once(later_column, pos, n, cap)
 
     def against(left, right):
         return lax.dot_general(left, right, (((1,), (1,)), ((), ())), preferred_element_type=F32)
@@ -519,7 +579,13 @@
     sigma = jax.nn.sigmoid(gate_pre)
     active = (gate_pre * sigma * up_pre).astype(BF)
 
-    logits, scale = row_sums(active, down_head, pos_own, weight_parts, label_count, depth, n, cap)
+    logits = row_sums(active, down_head, pos_own, weight_own, list(picked_later[:1]), label_count, depth, n, cap)
+    out_rows = column_product(
+        place, [(active, down_weight)], [pos_own, weight_parts], list(picked_later[:1]), one, depth, n, cap, width, "out_rows"
+    )[0]
+    crossed = send_core(out_rows[1])
+    out_dense = spread_back(out_rows, crossed, [], pos, 0, n, cap)
+    out_column = first_sum(out_dense)
     own_logits = lax.dot_general(
         own_head.astype(BF), hidden_in, (((1,), (1,)), ((), ())), preferred_element_type=F32
     )
@@ -532,7 +598,7 @@
 
     block = jnp.arange(depth * 2 * n).reshape(depth, 2 * n)
     logits = logits + jnp.where((block == 0)[..., None, None], own_logits, 0.0)
-    logits = turn(sum_all(turn(logits)))
+    logits = turn(sum_all(turn(logits), later[0][0] + later[0][1], across, depth))
     classes = (label_all[..., None, :] == jnp.arange(label_count, dtype=F32)[:, None]).astype(F32)
     powers = jnp.exp(logits)
     totals = jnp.sum(powers, axis=-2, keepdims=True)
@@ -545,29 +611,33 @@
         axis=2,
     )
 
-    def gradient_rows(b, value, features_ref, pos_ref, parts_ref):
-        chosen = own_selector(pos_ref, b, cap, tok_count)
-        parts = lax.dot_general(
-            chosen, parts_ref[0, b], (((1,), (1,)), ((), ())), preferred_element_type=F32
-        )
-        for k in range(label_count):
-            d_logit = parts[:, k : k + 1] + parts[:, label_count + k : label_count + k + 1]
-            value = value + d_logit * features_ref[1 + k : 2 + k, :]
+    keys = jnp.concatenate([all_features[1 : 1 + label_count]] * 2)
+    keys = jnp.concatenate([keys, jnp.zeros((16 - 2 * label_count, model_width), F32)]).astype(BF)
+
+    def gradient_rows(out_ref, keys_ref, pos_ref, parts_ref):
+        chosen = wide_selector(pos_ref, 2 * n, cap)
+        parts = jnp.concatenate([parts_ref[0, b] for b in range(2 * n)], axis=1)
+        picked = lax.dot_general(chosen, parts, (((1,), (1,)), ((), ())), preferred_element_type=F32)
         first = 2 * label_count
-        weight = parts[:, first : first + 1] + parts[:, first + 1 : first + 2] + parts[:, first + 2 : first + 3]
-        return (value.astype(BF).astype(F32) * weight).astype(BF)
+        weight = picked[:, first : first + 1] + picked[:, first + 1 : first + 2] + picked[:, first + 2 : first + 3]
+        head_term = jnp.dot(picked.astype(BF), keys_ref[...], preferred_element_type=F32)
+        for b in range(2 * n):
+            part = slice(b * cap, (b + 1) * cap)
+            value = head_term[part] + out_ref[0, b].astype(F32)
+            out_ref[0, b] = (value.astype(BF).astype(F32) * weight[part]).astype(BF)
 
     grads_in = assemble(
         place,
         later,
         one,
         gradient_rows,
-        [all_features, pos_own, d_parts],
+        [keys, pos_own, d_parts],
         [
-            whole_spec(all_features.shape),
+            whole_spec(keys.shape),
             pl.BlockSpec((1, 2 * n, 1, tok_count), lambda z, *_: (z, 0, 0, 0)),
             pl.BlockSpec((1, 2 * n, 16, tok_count), lambda z, *_: (z, 0, 0, 0)),
         ],
+        [crossed],
         model_width,
         "gradient_rows",
     ).reshape(row_count, model_width)
@@ -577,13 +647,17 @@
     d_up = (d_active * gate_pre * sigma).astype(BF)
 
     d_rows = column_product(
-        place, [(d_gate, gate_weight), (d_up, up_weight)], None, two, depth, n, cap, width, "d_rows"
-    )
-    d_normed = return_rows(d_rows, pos, two, across, cap)
-    out_rows = column_product(
-        place, [(active, down_weight)], scale, one, depth, n, cap, width, "out_rows"
-    )
-    mixed = return_rows(out_rows, pos, one, across, cap)
+        place, [(d_gate, gate_weight), (d_up, up_weight)], None, list(out_dense[:1]), two, depth, n, cap, width, "d_rows"
+    )
+    mixed = z_reduce(out_column, n)
+    d_column = [None] * depth
+    after = []
+    for rows, members in reversed(list(zip(d_rows, two))):
+        sums = first_sum(spread_back(rows, send_core(rows[1]), after, pos, members[0], n, cap))
+        after = [mixed, sums]
+        for i, k in enumerate(members):
+            d_column[k] = sums[i]
+    d_normed = z_reduce(d_column, n)
 
     grad_down = over_rows(active, grads_in)
     grad_gate = over_rows(d_gate, received)

time: 239 us -> 189 us (0.79)
  waiting for transfers between devices: 97.8 us -> 68.6 us
  starting transfers between devices: 69.2 us -> 52 us
  Pallas kernels: 32.5 us -> 27.9 us
    ppermute x52 -> x53, waiting for transfers between devices: 97.8 us -> 68.6 us  [send(): return lax.ppermute(value, ('ep', 'tp'), pairs)]
    ppermute x52 -> x53, starting transfers between devices: 69.2 us -> 52 us  [send(): return lax.ppermute(value, ('ep', 'tp'), pairs)]
    pallas_call x1, Pallas kernels: 5.05 us -> 1.85 us  [row_sums(): pl.pallas_call(body, grid=(depth,), in_specs=[pl.BlockSpec((1, 2 * n, cap...]
  transfers between devices with their start and end apart: 52 -> 53, of which waited for: 21 -> 26; matrix products, arithmetic and copies ran while one was open for 14% -> 18% of each run, Pallas kernels for 14% -> 13%
where the time goes in v1:
time: 189 us; the launch traced here: 188 us
  waiting for transfers between devices  68.6 us (36%)
  starting transfers between devices  52 us (28%)
  matrix products  29 us (15%)
  Pallas kernels  27.9 us (15%)
  other arithmetic  8.29 us (4%)
    ppermute x53, waiting for transfers between devices, send(): return lax.ppermute(value, ('ep', 'tp'), pairs)  68.6 us
    ppermute x53, starting transfers between devices, send(): return lax.ppermute(value, ('ep', 'tp'), pairs)  52 us
    pallas_call x2, Pallas kernels, column_product(): pl.pallas_call(body, grid_spec=pltpu.PrefetchScalarGridSpec(num_scalar_pr...  14.7 us
    dot_general x3, matrix products, over_rows(): lax.dot_general(left, right, (((0,), (0,)), ((), ())), preferred_element_...  12 us
    dot_general x3, matrix products, against(): lax.dot_general(left, right, (((1,), (1,)), ((), ())), preferred_element_...  11.5 us
    pallas_call x2, Pallas kernels, assemble(): pl.pallas_call(body, grid_spec=pltpu.PrefetchScalarGridSpec(num_scalar_pr...  5.97 us
  transfers between devices with their start and end apart: 53, of which 26 were waited for; matrix products, arithmetic and copies ran while one was open for 18% of the time, Pallas kernels for 13%

profile of v1, /device:TPU:0, one launch (start us, length us, event | category | flops | bytes accessed | tf_op | source)
XLA Modules:
  0.0 188.2 jit_solution(263045354516844362)
XLA Ops:
  2.8 4.0 %collective-permute-start.1 = (f32[24,128]{1,0:T(8,128)S(1)}, f32[24,128]{1,0:T(8,128)S(1)}, u32[]{:S(2)}, u32[]{:S(2)}) collective-permute-start(f32[24,128]{1,0:T(8,128)S(1)} %get-tuple-element.75), channel_id=1, source_target_pairs={{0,16},{1,17},{2,18},{3,19},{4,20},{5,21},{6,22},{7,23},{8,24},{9,... | collective-permute-start | bytes 36872 | tf_op jit(solution)/shard_map/ppermute | solution.py:36
  18.0 4.1 %collective-permute-done.2 = f32[24,128]{1,0:T(8,128)S(1)} collective-permute-done((f32[24,128]{1,0:T(8,128)S(1)}, f32[24,128]{1,0:T(8,128)S(1)}, u32[]{:S(2)}, u32[]{:S(2)}) %collective-permute-start.2) | collective-permute-done | bytes 12320 | tf_op jit(solution)/shard_map/ppermute | solution.py:36
  23.7 2.8 %fusion.35.head_ref = bf16[16,768]{1,0:T(8,128)(2,1)S(1)} fusion(bf16[768,2048]{1,0:T(8,128)(2,1)} %refs_1_.2, bf16[4,2048]{1,0:T(4,128)(2,1)S(1)} %bitcast.189, bf16[4,2048]{1,0:T(4,128)(2,1)S(1)} %broadcast_in_dim.65, pred[16]{0:T(512)(128)(4,1)S(1)} %iota_compare_fusion.5), kind=kOutput, calls=%fused_computation.94 | convolution fusion | flops 50655232 | bytes 3203088 | tf_op jit(solution)/shard_map/dot_general | solution.py:541
  31.7 3.4 %collective-permute-done.13.refs_2_ = bf16[128,1024]{1,0:T(8,128)(2,1)S(1)} collective-permute-done((bf16[128,1024]{1,0:T(8,128)(2,1)S(1)}, bf16[128,1024]{1,0:T(8,128)(2,1)S(1)}, u32[]{:S(2)}, u32[]{:S(2)}) %collective-permute-start.13) | collective-permute-done | bytes 262176 | tf_op jit(solution)/shard_map/ppermute | solution.py:36
  35.8 2.5 %collective-permute-start.22 = (bf16[128,1024]{1,0:T(8,128)(2,1)S(1)}, bf16[128,1024]{1,0:T(8,128)(2,1)S(1)}, u32[]{:S(2)}, u32[]{:S(2)}) collective-permute-start(bf16[128,1024]{1,0:T(8,128)(2,1)S(1)} %copy-done.5), channel_id=1, source_target_pairs={{0,8},{1,9},{2,10},{3,11},{4,12},{5,13},{6,14},{7,15},{8,0},{9,1},... | collective-permute-start | bytes 786440 | tf_op jit(solution)/shard_map/ppermute | solution.py:36
  45.1 6.5 %collective-permute-done.23 = bf16[128,1024]{1,0:T(8,128)(2,1)S(1)} collective-permute-done((bf16[128,1024]{1,0:T(8,128)(2,1)S(1)}, bf16[128,1024]{1,0:T(8,128)(2,1)S(1)}, u32[]{:S(2)}, u32[]{:S(2)}) %collective-permute-start.23) | collective-permute-done | bytes 262176 | tf_op jit(solution)/shard_map/ppermute | solution.py:36
  52.7 3.0 %collective-permute-done.18 = bf16[2,2,48,1024]{3,2,1,0:T(8,128)(2,1)S(1)} collective-permute-done((bf16[2,2,48,1024]{3,2,1,0:T(8,128)(2,1)S(1)}, bf16[2,2,48,1024]{3,2,1,0:T(8,128)(2,1)S(1)}, u32[]{:S(2)}, u32[]{:S(2)}) %collective-permute-start.18) | collective-permute-done | bytes 393248 | tf_op jit(solution)/shard_map/ppermute | solution.py:36
  57.2 3.3 %collective-permute-done.16.refs_5_ = bf16[2,2,48,1024]{3,2,1,0:T(8,128)(2,1)S(1)} collective-permute-done((bf16[2,2,48,1024]{3,2,1,0:T(8,128)(2,1)S(1)}, bf16[2,2,48,1024]{3,2,1,0:T(8,128)(2,1)S(1)}, u32[]{:S(2)}, u32[]{:S(2)}) %collective-permute-start.16) | collective-permute-done | bytes 393248 | tf_op jit(solution)/shard_map/ppermute | solution.py:36
  60.5 2.7 %normed_rows.1 = bf16[4,4,48,2048]{3,2,1,0:T(8,128)(2,1)S(1)} custom-call(s32[2]{0:T(128)S(1)} %pad_add_fusion.place_ref, bf16[2,2,48,1024]{3,2,1,0:T(8,128)(2,1)S(1)} %get-tuple-element.28.refs_0_, bf16[2,2,48,1024]{3,2,1,0:T(8,128)(2,1)S(1)} %collective-permute-done.7.refs_1_, bf16[2,2,48,1024]{3,2,1,0:T(8,128)(2,1)S(1)} %collective-permute-done.8.refs_2_, ...), custom_call_target="tpu_custom_call" | custom-call | flops 15728640 | bytes 6291456 | tf_op jit(solution)/shard_map/normed_rows/pallas_call | solution.py:217
  63.2 2.6 %fusion.76 = f32[768,768]{1,0:T(8,128)S(1)} fusion(bf16[768,2048]{1,0:T(8,128)(2,1)S(1)} %bitcast.166, bf16[768,2048]{1,0:T(8,128)(2,1)S(1)} %copy-done.3), kind=kOutput, calls=%fused_computation.162 | convolution fusion | flops 2415919104 | bytes 8650752 | tf_op jit(solution)/shard_map/dot_general | solution.py:572
  65.8 4.2 %multiply_convert_fusion.2 = (bf16[768,768]{1,0:T(8,128)(2,1)S(1)}, f32[768,768]{1,0:T(8,128)}) fusion(f32[768,768]{1,0:T(8,128)S(1)} %fusion.76, bf16[768,2048]{1,0:T(8,128)(2,1)S(1)} %bitcast.167, bf16[768,2048]{1,0:T(8,128)(2,1)S(1)} %copy-done.4), kind=kOutput, calls=%fused_computation.5 | convolution fusion | flops 2419458048 | bytes 12189696 | tf_op jit(solution)/shard_map/dot_general | solution.py:572
  74.5 6.6 %out_rows.1.refs_1_ = bf16[2,2,2,4,48,1024]{5,4,3,2,1,0:T(8,128)(2,1)S(1)} custom-call(s32[2]{0:T(128)S(1)} %pad_add_fusion.place_ref, bf16[4,4,48,768]{3,2,1,0:T(8,128)(2,1)S(1)} %bitcast.173, bf16[768,2048]{1,0:T(8,128)(2,1)S(1)} %copy-done.1, f32[4,4,1,128]{3,2,1,0:T(1,128)S(1)} %bitcast.180, bf16[4,4,16,128]{3,2,1,0:T(8,128)(2,1)S(1)} %maximum_maximum_fusion.refs_3_, ...), custom_call_target="tpu_custom_call" | custom-call | flops 2415919104 | bytes 7471104 | tf_op jit(solution)/shard_map/out_rows/pallas_call | solution.py:279
  85.7 3.0 %collective-permute-done.26 = f32[4,2,2,4,128]{4,3,2,1,0:T(4,128)S(1)} collective-permute-done((f32[4,2,2,4,128]{4,3,2,1,0:T(4,128)S(1)}, f32[4,2,2,4,128]{4,3,2,1,0:T(4,128)S(1)}, u32[]{:S(2)}, u32[]{:S(2)}) %collective-permute-start.26) | collective-permute-done | bytes 32800 | tf_op jit(solution)/shard_map/ppermute | solution.py:36
  90.6 3.4 %collective-permute-done.27 = f32[4,2,2,4,128]{4,3,2,1,0:T(4,128)S(1)} collective-permute-done((f32[4,2,2,4,128]{4,3,2,1,0:T(4,128)S(1)}, f32[4,2,2,4,128]{4,3,2,1,0:T(4,128)S(1)}, u32[]{:S(2)}, u32[]{:S(2)}) %collective-permute-start.27) | collective-permute-done | bytes 32800 | tf_op jit(solution)/shard_map/ppermute | solution.py:36
  100.7 7.1 %collective-permute-done.33 = f32[4,2,2,4,128]{4,3,2,1,0:T(4,128)S(1)} collective-permute-done((f32[4,2,2,4,128]{4,3,2,1,0:T(4,128)S(1)}, f32[4,2,2,4,128]{4,3,2,1,0:T(4,128)S(1)}, u32[]{:S(2)}, u32[]{:S(2)}) %collective-permute-start.33) | collective-permute-done | bytes 32800 | tf_op jit(solution)/shard_map/ppermute | solution.py:36
  108.0 3.3 %gradient_rows.1 = bf16[4,4,48,2048]{3,2,1,0:T(8,128)(2,1)S(1)} custom-call(s32[2]{0:T(128)S(1)} %pad_add_fusion.place_ref, bf16[2,4,48,1024]{3,2,1,0:T(8,128)(2,1)S(1)} %get-tuple-element.37.rest_0_.refs_4_.refs_0_, bf16[2,4,48,1024]{3,2,1,0:T(8,128)(2,1)S(1)} %collective-permute-done.28.refs_1_, ...), custom_call_target="tpu_custom_call" | custom-call | flops 15728640 | bytes 6291456 | tf_op jit(solution)/shard_map/gradient_rows/pallas_call | solution.py:217
  111.3 4.7 %multiply_convert_fusion = (bf16[768,768]{1,0:T(8,128)(2,1)S(1)}, bf16[768,768]{1,0:T(8,128)(2,1)S(1)}) fusion(f32[768,768]{1,0:T(8,128)S(1)} %fusion.76, f32[768,768]{1,0:T(8,128)} %get-tuple-element.81, bf16[768,2048]{1,0:T(8,128)(2,1)S(1)} %bitcast.170, bf16[768,2048]{1,0:T(8,128)(2,1)S(1)} %copy-done.1), kind=kOutput, calls=%fused_computation.3 | convolution fusion | flops 2423586816 | bytes 13369344 | tf_op jit(solution)/shard_map/dot_general | solution.py:572
  119.1 8.1 %d_rows.1 = (bf16[2,2,2,2,48,1024]{5,4,3,2,1,0:T(8,128)(2,1)S(1)}, bf16[2,2,2,2,48,1024]{5,4,3,2,1,0:T(8,128)(2,1)S(1)}) custom-call(s32[2]{0:T(128)S(1)} %pad_add_fusion.place_ref, bf16[4,4,48,768]{3,2,1,0:T(8,128)(2,1)S(1)} %bitcast.183, bf16[768,2048]{1,0:T(8,128)(2,1)S(1)} %copy-done.3, bf16[4,4,48,768]{3,2,1,0:T(8,128)(2,1)S(1)} %bitcast.182, ...), custom_call_target="tpu_custom_call" | custom-call | flops 4831838208 | bytes 11796480 | tf_op jit(solution)/shard_map/d_rows/pallas_call | solution.py:279
  131.0 3.8 %collective-permute-done.37 = bf16[4,128,1024]{2,1,0:T(8,128)(2,1)S(1)} collective-permute-done((bf16[4,128,1024]{2,1,0:T(8,128)(2,1)S(1)}, bf16[4,128,1024]{2,1,0:T(8,128)(2,1)S(1)}, u32[]{:S(2)}, u32[]{:S(2)}) %collective-permute-start.37) | collective-permute-done | bytes 1048608 | tf_op jit(solution)/shard_map/ppermute | solution.py:36
  136.3 4.0 %convolution_convert_fusion.2 = bf16[768,2048]{1,0:T(8,128)(2,1)} fusion(bf16[768,768]{1,0:T(8,128)(2,1)S(1)} %get-tuple-element.63, bf16[768,2048]{1,0:T(8,128)(2,1)S(1)} %bitcast.168), kind=kOutput, calls=%fused_computation.2 | convolution fusion | flops 2417491968 | bytes 7471104 | tf_op jit(solution)/shard_map/dot_general | solution.py:575
  148.1 10.2 %collective-permute-done.40 = bf16[128,1024]{1,0:T(8,128)(2,1)S(1)} collective-permute-done((bf16[128,1024]{1,0:T(8,128)(2,1)S(1)}, bf16[128,1024]{1,0:T(8,128)(2,1)S(1)}, u32[]{:S(2)}, u32[]{:S(2)}) %collective-permute-start.40) | collective-permute-done | bytes 262176 | tf_op jit(solution)/shard_map/ppermute | solution.py:36
  161.4 4.0 %convolution_convert_fusion.1 = bf16[768,2048]{1,0:T(8,128)(2,1)} fusion(bf16[768,768]{1,0:T(8,128)(2,1)S(1)} %get-tuple-element.62, bf16[768,2048]{1,0:T(8,128)(2,1)S(1)} %bitcast.169), kind=kOutput, calls=%fused_computation.1 | convolution fusion | flops 2417491968 | bytes 7471104 | tf_op jit(solution)/shard_map/dot_general | solution.py:575
  171.8 4.0 %convolution_convert_fusion = bf16[768,2048]{1,0:T(8,128)(2,1)} fusion(bf16[768,768]{1,0:T(8,128)(2,1)S(1)} %get-tuple-element.80, bf16[768,2048]{1,0:T(8,128)(2,1)S(1)} %bitcast.171), kind=kOutput, calls=%fused_computation | convolution fusion | flops 2417491968 | bytes 7471104 | tf_op jit(solution)/shard_map/dot_general | solution.py:575
  175.8 5.2 %collective-permute-done.51 = bf16[128,1024]{1,0:T(8,128)(2,1)S(1)} collective-permute-done((bf16[128,1024]{1,0:T(8,128)(2,1)S(1)}, bf16[128,1024]{1,0:T(8,128)(2,1)S(1)}, u32[]{:S(2)}, u32[]{:S(2)}) %collective-permute-start.51) | collective-permute-done | bytes 262176 | tf_op jit(solution)/shard_map/ppermute | solution.py:36
  (204 shorter events, 80.5 us)
Async XLA Ops:
  2.8 11.8 %collective-permute-start.1 = (f32[24,128]{1,0:T(8,128)S(1)}, f32[24,128]{1,0:T(8,128)S(1)}, u32[]{:S(2)}, u32[]{:S(2)}) collective-permute-start(f32[24,128]{1,0:T(8,128)S(1)} %get-tuple-element.75), channel_id=1, source_target_pairs={{0,16},{1,17},{2,18},{3,19},{4,20},{5,21},{6,22},{7,23},{8,24},{9,... | collective-permute-start | bytes 36872 | tf_op jit(solution)/shard_map/ppermute | solution.py:36
  8.4 27.4 %collective-permute-start.4 = (bf16[128,1024]{1,0:T(8,128)(2,1)}, bf16[128,1024]{1,0:T(8,128)(2,1)S(1)}, u32[]{:S(2)}, u32[]{:S(2)}) collective-permute-start(bf16[128,1024]{1,0:T(8,128)(2,1)} %refs_0_.1), channel_id=1, source_target_pairs={{0,4},{1,5},{2,3},{3,2},{4,0},{5,1},{6,7},{7,6},{8,12},{9,13},{10,... | collective-permute-start | bytes 786440 | tf_op jit(solution)/shard_map/ppermute | solution.py:36
  9.9 20.3 %collective-permute-start.5 = (bf16[128,1024]{1,0:T(8,128)(2,1)}, bf16[128,1024]{1,0:T(8,128)(2,1)S(1)}, u32[]{:S(2)}, u32[]{:S(2)}) collective-permute-start(bf16[128,1024]{1,0:T(8,128)(2,1)} %refs_0_.1), channel_id=1, source_target_pairs={{0,8},{1,9},{2,10},{3,11},{4,12},{5,13},{6,14},{7,15},{8,0},{9,1},... | collective-permute-start | bytes 786440 | tf_op jit(solution)/shard_map/ppermute | solution.py:36
  10.4 16.2 %collective-permute-start.11 = (bf16[128,1024]{1,0:T(8,128)(2,1)}, bf16[128,1024]{1,0:T(8,128)(2,1)S(1)}, u32[]{:S(2)}, u32[]{:S(2)}) collective-permute-start(bf16[128,1024]{1,0:T(8,128)(2,1)} %refs_0_.1), channel_id=1, source_target_pairs={{0,16},{1,17},{2,18},{3,19},{4,20},{5,21},{6,22},{7,23},{8,24},{9,... | collective-permute-start | bytes 786440 | tf_op jit(solution)/shard_map/ppermute | solution.py:36
  28.4 15.3 %collective-permute-start.15 = (bf16[128,1024]{1,0:T(8,128)(2,1)S(1)}, bf16[128,1024]{1,0:T(8,128)(2,1)S(1)}, u32[]{:S(2)}, u32[]{:S(2)}) collective-permute-start(bf16[128,1024]{1,0:T(8,128)(2,1)S(1)} %copy-done.5), channel_id=1, source_target_pairs={{0,16},{1,17},{2,18},{3,19},{4,20},{5,21},{6,22},{7,23},{8,24},{9,... | collective-permute-start | bytes 786440 | tf_op jit(solution)/shard_map/ppermute | solution.py:36
  39.4 12.8 %collective-permute-start.7 = (bf16[2,2,48,1024]{3,2,1,0:T(8,128)(2,1)S(1)}, bf16[2,2,48,1024]{3,2,1,0:T(8,128)(2,1)S(1)}, u32[]{:S(2)}, u32[]{:S(2)}) collective-permute-start(bf16[2,2,48,1024]{3,2,1,0:T(8,128)(2,1)S(1)} %get-tuple-element.29), channel_id=1, source_target_pairs={{0,1},{1,0},{2,6},{3,7},{4,5},{5,4},{6,2},{7,3},{8,9},{9,8},{10,14... | collective-permute-start | bytes 1179656 | tf_op jit(solution)/shard_map/ppermute | solution.py:36
  40.1 12.1 %collective-permute-start.9 = (bf16[2,2,48,1024]{3,2,1,0:T(8,128)(2,1)S(1)}, bf16[2,2,48,1024]{3,2,1,0:T(8,128)(2,1)S(1)}, u32[]{:S(2)}, u32[]{:S(2)}) collective-permute-start(bf16[2,2,48,1024]{3,2,1,0:T(8,128)(2,1)S(1)} %get-tuple-element.31), channel_id=1, source_target_pairs={{0,1},{1,0},{2,6},{3,7},{4,5},{5,4},{6,2},{7,3},{8,9},{9,8},{10,14... | collective-permute-start | bytes 1179656 | tf_op jit(solution)/shard_map/ppermute | solution.py:36
  44.3 11.4 %collective-permute-start.18 = (bf16[2,2,48,1024]{3,2,1,0:T(8,128)(2,1)S(1)}, bf16[2,2,48,1024]{3,2,1,0:T(8,128)(2,1)S(1)}, u32[]{:S(2)}, u32[]{:S(2)}) collective-permute-start(bf16[2,2,48,1024]{3,2,1,0:T(8,128)(2,1)S(1)} %get-tuple-element.36), channel_id=1, source_target_pairs={{0,1},{1,0},{2,6},{3,7},{4,5},{5,4},{6,2},{7,3},{8,9},{9,8},{10,14... | collective-permute-start | bytes 1179656 | tf_op jit(solution)/shard_map/ppermute | solution.py:36
  56.1 14.9 %collective-permute-start.24 = (bf16[4,128,1024]{2,1,0:T(8,128)(2,1)S(1)}, bf16[4,128,1024]{2,1,0:T(8,128)(2,1)S(1)}, u32[]{:S(2)}, u32[]{:S(2)}) collective-permute-start(bf16[4,128,1024]{2,1,0:T(8,128)(2,1)S(1)} %pad_maximum_fusion.refs_0_), channel_id=1, source_target_pairs={{0,4},{1,5},{2,3},{3,2},{4,0},{5,1},{6,7},{7,6},{8,12},{9,13},{10,... | collective-permute-start | bytes 3145736 | tf_op jit(solution)/shard_map/ppermute | solution.py:36
  71.9 12.1 %collective-permute-start.30 = (bf16[2,4,48,1024]{3,2,1,0:T(8,128)(2,1)S(1)}, bf16[2,4,48,1024]{3,2,1,0:T(8,128)(2,1)S(1)}, u32[]{:S(2)}, u32[]{:S(2)}) collective-permute-start(bf16[2,4,48,1024]{3,2,1,0:T(8,128)(2,1)S(1)} %get-tuple-element.40), channel_id=1, source_target_pairs={{0,1},{1,0},{2,6},{3,7},{4,5},{5,4},{6,2},{7,3},{8,9},{9,8},{10,14... | collective-permute-start | bytes 2359304 | tf_op jit(solution)/shard_map/ppermute | solution.py:36
  81.3 18.6 %collective-permute-start.34 = (bf16[2,2,4,48,1024]{4,3,2,1,0:T(8,128)(2,1)S(1)}, bf16[2,2,4,48,1024]{4,3,2,1,0:T(8,128)(2,1)S(1)}, u32[]{:S(2)}, u32[]{:S(2)}) collective-permute-start(bf16[2,2,4,48,1024]{4,3,2,1,0:T(8,128)(2,1)S(1)} %slice_bitcast_fusion), channel_id=1, source_target_pairs={{0,2},{1,3},{2,0},{3,1},{4,6},{5,7},{6,4},{7,5},{8,10},{9,11},{10,... | collective-permute-start | bytes 4718600 | tf_op jit(solution)/shard_map/ppermute | solution.py:36
  82.1 12.0 %collective-permute-start.28 = (bf16[2,4,48,1024]{3,2,1,0:T(8,128)(2,1)S(1)}, bf16[2,4,48,1024]{3,2,1,0:T(8,128)(2,1)S(1)}, u32[]{:S(2)}, u32[]{:S(2)}) collective-permute-start(bf16[2,4,48,1024]{3,2,1,0:T(8,128)(2,1)S(1)} %get-tuple-element.38), channel_id=1, source_target_pairs={{0,1},{1,0},{2,6},{3,7},{4,5},{5,4},{6,2},{7,3},{8,9},{9,8},{10,14... | collective-permute-start | bytes 2359304 | tf_op jit(solution)/shard_map/ppermute | solution.py:36
  95.0 21.0 %collective-permute-start.35 = (bf16[2,4,48,1024]{3,2,1,0:T(8,128)(2,1)S(1)}, bf16[2,4,48,1024]{3,2,1,0:T(8,128)(2,1)S(1)}, u32[]{:S(2)}, u32[]{:S(2)}) collective-permute-start(bf16[2,4,48,1024]{3,2,1,0:T(8,128)(2,1)S(1)} %slice_bitcast_fusion.2), channel_id=1, source_target_pairs={{0,1},{1,0},{2,6},{3,7},{4,5},{5,4},{6,2},{7,3},{8,9},{9,8},{10,14... | collective-permute-start | bytes 2359304 | tf_op jit(solution)/shard_map/ppermute | solution.py:36
  100.0 16.2 %collective-permute-start.36 = (bf16[2,4,48,1024]{3,2,1,0:T(8,128)(2,1)S(1)}, bf16[2,4,48,1024]{3,2,1,0:T(8,128)(2,1)S(1)}, u32[]{:S(2)}, u32[]{:S(2)}) collective-permute-start(bf16[2,4,48,1024]{3,2,1,0:T(8,128)(2,1)S(1)} %slice_bitcast_fusion.1), channel_id=1, source_target_pairs={{0,1},{1,0},{2,6},{3,7},{4,5},{5,4},{6,2},{7,3},{8,9},{9,8},{10,14... | collective-permute-start | bytes 2359304 | tf_op jit(solution)/shard_map/ppermute | solution.py:36
  117.8 16.9 %collective-permute-start.37 = (bf16[4,128,1024]{2,1,0:T(8,128)(2,1)S(1)}, bf16[4,128,1024]{2,1,0:T(8,128)(2,1)S(1)}, u32[]{:S(2)}, u32[]{:S(2)}) collective-permute-start(bf16[4,128,1024]{2,1,0:T(8,128)(2,1)S(1)} %get-tuple-element.43), channel_id=1, source_target_pairs={{0,4},{1,5},{2,3},{3,2},{4,0},{5,1},{6,7},{7,6},{8,12},{9,13},{10,... | collective-permute-start | bytes 3145736 | tf_op jit(solution)/shard_map/ppermute | solution.py:36
  127.4 14.0 %collective-permute-start.45 = (bf16[2,2,48,1024]{3,2,1,0:T(8,128)(2,1)S(1)}, bf16[2,2,48,1024]{3,2,1,0:T(8,128)(2,1)S(1)}, u32[]{:S(2)}, u32[]{:S(2)}) collective-permute-start(bf16[2,2,48,1024]{3,2,1,0:T(8,128)(2,1)S(1)} %slice_bitcast_fusion.11), channel_id=1, source_target_pairs={{0,1},{1,0},{2,6},{3,7},{4,5},{5,4},{6,2},{7,3},{8,9},{9,8},{10,14... | collective-permute-start | bytes 1179656 | tf_op jit(solution)/shard_map/ppermute | solution.py:36
  128.8 18.3 %collective-permute-start.41 = (bf16[2,2,2,48,1024]{4,3,2,1,0:T(8,128)(2,1)S(1)}, bf16[2,2,2,48,1024]{4,3,2,1,0:T(8,128)(2,1)S(1)}, u32[]{:S(2)}, u32[]{:S(2)}) collective-permute-start(bf16[2,2,2,48,1024]{4,3,2,1,0:T(8,128)(2,1)S(1)} %slice_bitcast_fusion.4), channel_id=1, source_target_pairs={{0,2},{1,3},{2,0},{3,1},{4,6},{5,7},{6,4},{7,5},{8,10},{9,11},{10,... | collective-permute-start | bytes 2359304 | tf_op jit(solution)/shard_map/ppermute | solution.py:36
  129.6 11.7 %collective-permute-start.46 = (bf16[2,2,48,1024]{3,2,1,0:T(8,128)(2,1)S(1)}, bf16[2,2,48,1024]{3,2,1,0:T(8,128)(2,1)S(1)}, u32[]{:S(2)}, u32[]{:S(2)}) collective-permute-start(bf16[2,2,48,1024]{3,2,1,0:T(8,128)(2,1)S(1)} %slice_bitcast_fusion.9), channel_id=1, source_target_pairs={{0,1},{1,0},{2,6},{3,7},{4,5},{5,4},{6,2},{7,3},{8,9},{9,8},{10,14... | collective-permute-start | bytes 1179656 | tf_op jit(solution)/shard_map/ppermute | solution.py:36
  142.3 16.8 %collective-permute-start.47 = (bf16[2,128,1024]{2,1,0:T(8,128)(2,1)S(1)}, bf16[2,128,1024]{2,1,0:T(8,128)(2,1)S(1)}, u32[]{:S(2)}, u32[]{:S(2)}) collective-permute-start(bf16[2,128,1024]{2,1,0:T(8,128)(2,1)S(1)} %get-tuple-element.47), channel_id=1, source_target_pairs={{0,4},{1,5},{2,3},{3,2},{4,0},{5,1},{6,7},{7,6},{8,12},{9,13},{10,... | collective-permute-start | bytes 1572872 | tf_op jit(solution)/shard_map/ppermute | solution.py:36
  144.1 14.2 %collective-permute-start.40 = (bf16[128,1024]{1,0:T(8,128)(2,1)S(1)}, bf16[128,1024]{1,0:T(8,128)(2,1)S(1)}, u32[]{:S(2)}, u32[]{:S(2)}) collective-permute-start(bf16[128,1024]{1,0:T(8,128)(2,1)S(1)} %fusion.13), channel_id=1, source_target_pairs={{0,16},{1,17},{2,18},{3,19},{4,20},{5,21},{6,22},{7,23},{8,24},{9,... | collective-permute-start | bytes 786440 | tf_op jit(solution)/shard_map/ppermute | solution.py:36
  145.9 13.5 %collective-permute-start.42 = (bf16[2,2,48,1024]{3,2,1,0:T(8,128)(2,1)S(1)}, bf16[2,2,48,1024]{3,2,1,0:T(8,128)(2,1)S(1)}, u32[]{:S(2)}, u32[]{:S(2)}) collective-permute-start(bf16[2,2,48,1024]{3,2,1,0:T(8,128)(2,1)S(1)} %slice_bitcast_fusion.12), channel_id=1, source_target_pairs={{0,1},{1,0},{2,6},{3,7},{4,5},{5,4},{6,2},{7,3},{8,9},{9,8},{10,14... | collective-permute-start | bytes 1179656 | tf_op jit(solution)/shard_map/ppermute | solution.py:36
  147.2 12.2 %collective-permute-start.43 = (bf16[2,2,48,1024]{3,2,1,0:T(8,128)(2,1)S(1)}, bf16[2,2,48,1024]{3,2,1,0:T(8,128)(2,1)S(1)}, u32[]{:S(2)}, u32[]{:S(2)}) collective-permute-start(bf16[2,2,48,1024]{3,2,1,0:T(8,128)(2,1)S(1)} %slice_bitcast_fusion.10), channel_id=1, source_target_pairs={{0,1},{1,0},{2,6},{3,7},{4,5},{5,4},{6,2},{7,3},{8,9},{9,8},{10,14... | collective-permute-start | bytes 1179656 | tf_op jit(solution)/shard_map/ppermute | solution.py:36
  167.1 13.9 %collective-permute-start.51 = (bf16[128,1024]{1,0:T(8,128)(2,1)S(1)}, bf16[128,1024]{1,0:T(8,128)(2,1)S(1)}, u32[]{:S(2)}, u32[]{:S(2)}) collective-permute-start(bf16[128,1024]{1,0:T(8,128)(2,1)S(1)} %fusion.8), channel_id=1, source_target_pairs={{0,16},{1,17},{2,18},{3,19},{4,20},{5,21},{6,22},{7,23},{8,24},{9,... | collective-permute-start | bytes 786440 | tf_op jit(solution)/shard_map/ppermute | solution.py:36
  169.8 13.2 %collective-permute-start.49 = (bf16[128,1024]{1,0:T(8,128)(2,1)S(1)}, bf16[128,1024]{1,0:T(8,128)(2,1)S(1)}, u32[]{:S(2)}, u32[]{:S(2)}) collective-permute-start(bf16[128,1024]{1,0:T(8,128)(2,1)S(1)} %fusion.16), channel_id=1, source_target_pairs={{0,8},{1,9},{2,10},{3,11},{4,12},{5,13},{6,14},{7,15},{8,0},{9,1},... | collective-permute-start | bytes 786440 | tf_op jit(solution)/shard_map/ppermute | solution.py:36
  (38 other events, 346.1 us)

commit v2 on v1

--- a/solution.py
+++ b/solution.py
@@ -110,7 +110,7 @@
     return jnp.concatenate(parts, axis=0).astype(BF)
 
 
-def pick_rows(units, after, pos, start, cap):
+def pick_rows(units, after, pos, start, cap, joined=False):
     n, _, experts, tokens = pos.shape
     stacked = not isinstance(units[0], (list, tuple))
     group = units[0].shape[0] if stacked else len(units)
@@ -118,21 +118,27 @@
     width = flat[0].shape[-1]
 
     def body(pos_ref, *refs):
-        ins, outs = refs[: len(flat)], refs[-experts:]
+        ins, outs = refs[: len(flat)], refs[len(flat) + len(after) :]
         for z in range(group):
             for h in range(n):
                 chosen = selector(pos_ref, h, start + z, cap, experts, tokens)
                 unit = ins[h][z] if stacked else ins[z * n + h][...]
                 rows = jnp.dot(chosen, unit, preferred_element_type=F32).astype(BF)
                 for e in range(experts):
-                    outs[e][h, z] = rows[e * cap : (e + 1) * cap]
+                    part = rows[e * cap : (e + 1) * cap]
+                    if joined:
+                        outs[e // 2][e % 2, h, z] = part
+                    else:
+                        outs[e][h, z] = part
 
     vmem = pl.BlockSpec(memory_space=pltpu.VMEM)
     return pl.pallas_call(
         body,
         in_specs=[vmem] * (1 + len(flat)) + [pl.BlockSpec(memory_space=pl.ANY)] * len(after),
-        out_specs=[vmem] * experts,
-        out_shape=[jax.ShapeDtypeStruct((n, group, cap, width), BF)] * experts,
+        out_specs=[vmem] * (n if joined else experts),
+        out_shape=[jax.ShapeDtypeStruct((2, n, group, cap, width), BF)] * n
+        if joined
+        else [jax.ShapeDtypeStruct((n, group, cap, width), BF)] * experts,
         compiler_params=params(),
         cost_estimate=pl.CostEstimate(
             flops=2 * group * n * experts * cap * tokens * width,
@@ -364,15 +370,19 @@
     )(active.reshape(depth, 2 * n, cap, units), down_head, pos_own, weight_own, *after)
 
 
-def route_rows(units, after, pos, start, cap):
-    rows = pick_rows(units, after, pos, start, cap)
+def route_rows(units, after, pos, start, cap, joined=False):
+    rows = pick_rows(units, after, pos, start, cap, joined)
     n = pos.shape[0]
     here, other = [], []
     for f in range(n):
-        same, cross = rows[2 * f], rows[2 * f + 1]
-        if f > 0:
-            cross = send_last(cross, f)
-            same = send_last(same, f)
+        if joined:
+            both = rows[f] if f == 0 else send_last(rows[f], f)
+            same, cross = both[0], both[1]
+        else:
+            same, cross = rows[2 * f], rows[2 * f + 1]
+            if f > 0:
+                cross = send_last(cross, f)
+                same = send_last(same, f)
         here.append(same)
         other.append(send_core(cross))
     return [here, other], rows
@@ -390,7 +400,7 @@
 def pick_at_once(column, pos, n, cap):
     column = jnp.stack(column)
     units = [column] + [send_first(column, k) for k in range(1, n)]
-    pieces, rows = route_rows(units, [], pos, 0, cap)
+    pieces, rows = route_rows(units, [], pos, 0, cap, True)
     return [pieces], rows
 
 

time: 189 us -> 186 us (0.984)
  waiting for transfers between devices: 68.6 us -> 71.4 us
  matrix products: 29 us -> 26.3 us
  starting transfers between devices: 52 us -> 49.4 us
    ppermute x53 -> x52, waiting for transfers between devices: 68.6 us -> 71.4 us  [send(): return lax.ppermute(value, ('ep', 'tp'), pairs)]
    dot_general x3, matrix products: 11.5 us -> 8.74 us  [against(): lax.dot_general(left, right, (((1,), (1,)), ((), ())), preferred_element_...]
    ppermute x53 -> x52, starting transfers between devices: 52 us -> 49.4 us  [send(): return lax.ppermute(value, ('ep', 'tp'), pairs)]
  transfers between devices with their start and end apart: 53 -> 52, of which waited for: 26 -> 24; matrix products, arithmetic and copies ran while one was open for 18% -> 17% of each run, Pallas kernels for 13% -> 14%
where the time goes in v2:
time: 186 us
  waiting for transfers between devices  71.4 us (38%)
  starting transfers between devices  49.4 us (27%)
  Pallas kernels  27.9 us (15%)
  matrix products  26.3 us (14%)
  other arithmetic  8.31 us (4%)
    ppermute x52, waiting for transfers between devices, send(): return lax.ppermute(value, ('ep', 'tp'), pairs)  71.4 us
    ppermute x52, starting transfers between devices, send(): return lax.ppermute(value, ('ep', 'tp'), pairs)  49.4 us
    pallas_call x2, Pallas kernels, column_product(): pl.pallas_call(body, grid_spec=pltpu.PrefetchScalarGridSpec(num_scalar_pr...  14.7 us
    dot_general x3, matrix products, over_rows(): lax.dot_general(left, right, (((0,), (0,)), ((), ())), preferred_element_...  12 us
    dot_general x3, matrix products, against(): lax.dot_general(left, right, (((1,), (1,)), ((), ())), preferred_element_...  8.74 us
    pallas_call x2, Pallas kernels, assemble(): pl.pallas_call(body, grid_spec=pltpu.PrefetchScalarGridSpec(num_scalar_pr...  5.96 us
  transfers between devices with their start and end apart: 52, of which 24 were waited for; matrix products, arithmetic and copies ran while one was open for 17% of the time, Pallas kernels for 14%

profile of v2, /device:TPU:0, one launch (start us, length us, event | category | flops | bytes accessed | tf_op | source)
XLA Modules:
  0.0 185.9 jit_solution(13731564825473019319)
XLA Ops:
  2.8 4.0 %collective-permute-start.1 = (f32[24,128]{1,0:T(8,128)S(1)}, f32[24,128]{1,0:T(8,128)S(1)}, u32[]{:S(2)}, u32[]{:S(2)}) collective-permute-start(f32[24,128]{1,0:T(8,128)S(1)} %get-tuple-element.75), channel_id=1, source_target_pairs={{0,16},{1,17},{2,18},{3,19},{4,20},{5,21},{6,22},{7,23},{8,24},{9,... | collective-permute-start | bytes 36872 | tf_op jit(solution)/shard_map/ppermute | solution.py:36
  18.0 4.1 %collective-permute-done.2 = f32[24,128]{1,0:T(8,128)S(1)} collective-permute-done((f32[24,128]{1,0:T(8,128)S(1)}, f32[24,128]{1,0:T(8,128)S(1)}, u32[]{:S(2)}, u32[]{:S(2)}) %collective-permute-start.2) | collective-permute-done | bytes 12320 | tf_op jit(solution)/shard_map/ppermute | solution.py:36
  23.7 2.8 %fusion.35.head_ref = bf16[16,768]{1,0:T(8,128)(2,1)S(1)} fusion(bf16[768,2048]{1,0:T(8,128)(2,1)} %refs_1_.2, bf16[4,2048]{1,0:T(4,128)(2,1)S(1)} %bitcast.197, bf16[4,2048]{1,0:T(4,128)(2,1)S(1)} %broadcast_in_dim.65, pred[16]{0:T(512)(128)(4,1)S(1)} %iota_compare_fusion.5), kind=kOutput, calls=%fused_computation.98 | convolution fusion | flops 50655232 | bytes 3203088 | tf_op jit(solution)/shard_map/dot_general | solution.py:551
  31.7 3.4 %collective-permute-done.13.refs_2_ = bf16[128,1024]{1,0:T(8,128)(2,1)S(1)} collective-permute-done((bf16[128,1024]{1,0:T(8,128)(2,1)S(1)}, bf16[128,1024]{1,0:T(8,128)(2,1)S(1)}, u32[]{:S(2)}, u32[]{:S(2)}) %collective-permute-start.13) | collective-permute-done | bytes 262176 | tf_op jit(solution)/shard_map/ppermute | solution.py:36
  45.1 6.5 %collective-permute-done.23 = bf16[128,1024]{1,0:T(8,128)(2,1)S(1)} collective-permute-done((bf16[128,1024]{1,0:T(8,128)(2,1)S(1)}, bf16[128,1024]{1,0:T(8,128)(2,1)S(1)}, u32[]{:S(2)}, u32[]{:S(2)}) %collective-permute-start.23) | collective-permute-done | bytes 262176 | tf_op jit(solution)/shard_map/ppermute | solution.py:36
  52.7 3.0 %collective-permute-done.18 = bf16[2,2,48,1024]{3,2,1,0:T(8,128)(2,1)S(1)} collective-permute-done((bf16[2,2,48,1024]{3,2,1,0:T(8,128)(2,1)S(1)}, bf16[2,2,48,1024]{3,2,1,0:T(8,128)(2,1)S(1)}, u32[]{:S(2)}, u32[]{:S(2)}) %collective-permute-start.18) | collective-permute-done | bytes 393248 | tf_op jit(solution)/shard_map/ppermute | solution.py:36
  57.2 3.3 %collective-permute-done.16.refs_5_ = bf16[2,2,48,1024]{3,2,1,0:T(8,128)(2,1)S(1)} collective-permute-done((bf16[2,2,48,1024]{3,2,1,0:T(8,128)(2,1)S(1)}, bf16[2,2,48,1024]{3,2,1,0:T(8,128)(2,1)S(1)}, u32[]{:S(2)}, u32[]{:S(2)}) %collective-permute-start.16) | collective-permute-done | bytes 393248 | tf_op jit(solution)/shard_map/ppermute | solution.py:36
  60.5 2.7 %normed_rows.1 = bf16[4,4,48,2048]{3,2,1,0:T(8,128)(2,1)S(1)} custom-call(s32[2]{0:T(128)S(1)} %pad_add_fusion.place_ref, bf16[2,2,48,1024]{3,2,1,0:T(8,128)(2,1)S(1)} %get-tuple-element.26.refs_0_, bf16[2,2,48,1024]{3,2,1,0:T(8,128)(2,1)S(1)} %collective-permute-done.7.refs_1_, bf16[2,2,48,1024]{3,2,1,0:T(8,128)(2,1)S(1)} %collective-permute-done.8.refs_2_, ...), custom_call_target="tpu_custom_call" | custom-call | flops 15728640 | bytes 6291456 | tf_op jit(solution)/shard_map/normed_rows/pallas_call | solution.py:223
  63.2 2.6 %fusion.76 = f32[768,768]{1,0:T(8,128)S(1)} fusion(bf16[768,2048]{1,0:T(8,128)(2,1)S(1)} %bitcast.176, bf16[768,2048]{1,0:T(8,128)(2,1)S(1)} %copy-done.3), kind=kOutput, calls=%fused_computation.166 | convolution fusion | flops 2415919104 | bytes 8650752 | tf_op jit(solution)/shard_map/dot_general | solution.py:582
  65.8 2.8 %multiply_convert_fusion.2 = (bf16[768,768]{1,0:T(8,128)(2,1)S(1)}, f32[768,768]{1,0:T(8,128)S(1)}) fusion(f32[768,768]{1,0:T(8,128)S(1)} %fusion.76, bf16[768,2048]{1,0:T(8,128)(2,1)S(1)} %bitcast.177, bf16[768,2048]{1,0:T(8,128)(2,1)S(1)} %copy-done.4), kind=kOutput, calls=%fused_computation.5 | convolution fusion | flops 2419458048 | bytes 12189696 | tf_op jit(solution)/shard_map/dot_general | solution.py:582
  74.5 6.6 %out_rows.1.refs_1_ = bf16[2,2,2,4,48,1024]{5,4,3,2,1,0:T(8,128)(2,1)S(1)} custom-call(s32[2]{0:T(128)S(1)} %pad_add_fusion.place_ref, bf16[4,4,48,768]{3,2,1,0:T(8,128)(2,1)S(1)} %bitcast.175, bf16[768,2048]{1,0:T(8,128)(2,1)S(1)} %copy-done, f32[4,4,1,128]{3,2,1,0:T(1,128)S(1)} %bitcast.188, bf16[4,4,16,128]{3,2,1,0:T(8,128)(2,1)S(1)} %maximum_maximum_fusion.refs_3_, ...), custom_call_target="tpu_custom_call" | custom-call | flops 2415919104 | bytes 7471104 | tf_op jit(solution)/shard_map/out_rows/pallas_call | solution.py:285
  83.8 8.5 %collective-permute-done.28 = bf16[2,2,4,48,1024]{4,3,2,1,0:T(8,128)(2,1)S(1)} collective-permute-done((bf16[2,2,4,48,1024]{4,3,2,1,0:T(8,128)(2,1)S(1)}, bf16[2,2,4,48,1024]{4,3,2,1,0:T(8,128)(2,1)S(1)}, u32[]{:S(2)}, u32[]{:S(2)}) %collective-permute-start.28) | collective-permute-done | bytes 1572896 | tf_op jit(solution)/shard_map/ppermute | solution.py:36
  94.3 3.0 %collective-permute-done.26 = f32[4,2,2,4,128]{4,3,2,1,0:T(4,128)S(1)} collective-permute-done((f32[4,2,2,4,128]{4,3,2,1,0:T(4,128)S(1)}, f32[4,2,2,4,128]{4,3,2,1,0:T(4,128)S(1)}, u32[]{:S(2)}, u32[]{:S(2)}) %collective-permute-start.26) | collective-permute-done | bytes 32800 | tf_op jit(solution)/shard_map/ppermute | solution.py:36
  99.3 3.3 %collective-permute-done.27 = f32[4,2,2,4,128]{4,3,2,1,0:T(4,128)S(1)} collective-permute-done((f32[4,2,2,4,128]{4,3,2,1,0:T(4,128)S(1)}, f32[4,2,2,4,128]{4,3,2,1,0:T(4,128)S(1)}, u32[]{:S(2)}, u32[]{:S(2)}) %collective-permute-start.27) | collective-permute-done | bytes 32800 | tf_op jit(solution)/shard_map/ppermute | solution.py:36
  103.5 3.5 %collective-permute-done.31 = f32[4,2,2,4,128]{4,3,2,1,0:T(4,128)S(1)} collective-permute-done((f32[4,2,2,4,128]{4,3,2,1,0:T(4,128)S(1)}, f32[4,2,2,4,128]{4,3,2,1,0:T(4,128)S(1)}, u32[]{:S(2)}, u32[]{:S(2)}) %collective-permute-start.31) | collective-permute-done | bytes 32800 | tf_op jit(solution)/shard_map/ppermute | solution.py:36
  112.2 3.3 %gradient_rows.1 = bf16[4,4,48,2048]{3,2,1,0:T(8,128)(2,1)S(1)} custom-call(s32[2]{0:T(128)S(1)} %pad_add_fusion.place_ref, bf16[2,4,48,1024]{3,2,1,0:T(8,128)(2,1)S(1)} %get-tuple-element.65.refs_0_, bf16[2,4,48,1024]{3,2,1,0:T(8,128)(2,1)S(1)} %get-tuple-element.63.refs_1_, bf16[2,4,48,1024]{3,2,1,0:T(8,128)(2,1)S(1)} %collective-permute-done.29.refs_2_, ...), custom_call_target="tpu_custom_call" | custom-call | flops 15728640 | bytes 6291456 | tf_op jit(solution)/shard_map/gradient_rows/pallas_call | solution.py:223
  115.5 3.3 %multiply_convert_fusion = (bf16[768,768]{1,0:T(8,128)(2,1)S(1)}, bf16[768,768]{1,0:T(8,128)(2,1)S(1)}) fusion(f32[768,768]{1,0:T(8,128)S(1)} %fusion.76, f32[768,768]{1,0:T(8,128)S(1)} %get-tuple-element.81, bf16[768,2048]{1,0:T(8,128)(2,1)S(1)} %bitcast.180, bf16[768,2048]{1,0:T(8,128)(2,1)S(1)} %copy-done), kind=kOutput, calls=%fused_computation.3 | convolution fusion | flops 2423586816 | bytes 13369344 | tf_op jit(solution)/shard_map/dot_general | solution.py:582
  118.8 8.0 %d_rows.1 = (bf16[2,2,2,2,48,1024]{5,4,3,2,1,0:T(8,128)(2,1)S(1)}, bf16[2,2,2,2,48,1024]{5,4,3,2,1,0:T(8,128)(2,1)S(1)}) custom-call(s32[2]{0:T(128)S(1)} %pad_add_fusion.place_ref, bf16[4,4,48,768]{3,2,1,0:T(8,128)(2,1)S(1)} %bitcast.191, bf16[768,2048]{1,0:T(8,128)(2,1)S(1)} %copy-done.3, bf16[4,4,48,768]{3,2,1,0:T(8,128)(2,1)S(1)} %bitcast.190, ...), custom_call_target="tpu_custom_call" | custom-call | flops 4831838208 | bytes 11796480 | tf_op jit(solution)/shard_map/d_rows/pallas_call | solution.py:285
  131.5 4.0 %convolution_convert_fusion.2 = bf16[768,2048]{1,0:T(8,128)(2,1)} fusion(bf16[768,768]{1,0:T(8,128)(2,1)S(1)} %get-tuple-element.59, bf16[768,2048]{1,0:T(8,128)(2,1)S(1)} %bitcast.178), kind=kOutput, calls=%fused_computation.2 | convolution fusion | flops 2417491968 | bytes 7471104 | tf_op jit(solution)/shard_map/dot_general | solution.py:585
  136.7 2.9 %collective-permute-done.45.refs_4_ = bf16[2,2,48,1024]{3,2,1,0:T(8,128)(2,1)S(1)} collective-permute-done((bf16[2,2,48,1024]{3,2,1,0:T(8,128)(2,1)S(1)}, bf16[2,2,48,1024]{3,2,1,0:T(8,128)(2,1)S(1)}, u32[]{:S(2)}, u32[]{:S(2)}) %collective-permute-start.45) | collective-permute-done | bytes 393248 | tf_op jit(solution)/shard_map/ppermute | solution.py:36
  147.6 7.3 %collective-permute-done.39 = bf16[128,1024]{1,0:T(8,128)(2,1)S(1)} collective-permute-done((bf16[128,1024]{1,0:T(8,128)(2,1)S(1)}, bf16[128,1024]{1,0:T(8,128)(2,1)S(1)}, u32[]{:S(2)}, u32[]{:S(2)}) %collective-permute-start.39) | collective-permute-done | bytes 262176 | tf_op jit(solution)/shard_map/ppermute | solution.py:36
  158.3 4.0 %convolution_convert_fusion.1 = bf16[768,2048]{1,0:T(8,128)(2,1)} fusion(bf16[768,768]{1,0:T(8,128)(2,1)S(1)} %get-tuple-element.58, bf16[768,2048]{1,0:T(8,128)(2,1)S(1)} %bitcast.179), kind=kOutput, calls=%fused_computation.1 | convolution fusion | flops 2417491968 | bytes 7471104 | tf_op jit(solution)/shard_map/dot_general | solution.py:585
  168.6 4.0 %convolution_convert_fusion = bf16[768,2048]{1,0:T(8,128)(2,1)} fusion(bf16[768,768]{1,0:T(8,128)(2,1)S(1)} %get-tuple-element.80, bf16[768,2048]{1,0:T(8,128)(2,1)S(1)} %bitcast.181), kind=kOutput, calls=%fused_computation | convolution fusion | flops 2417491968 | bytes 7471104 | tf_op jit(solution)/shard_map/dot_general | solution.py:585
  172.6 5.6 %collective-permute-done.50 = bf16[128,1024]{1,0:T(8,128)(2,1)S(1)} collective-permute-done((bf16[128,1024]{1,0:T(8,128)(2,1)S(1)}, bf16[128,1024]{1,0:T(8,128)(2,1)S(1)}, u32[]{:S(2)}, u32[]{:S(2)}) %collective-permute-start.50) | collective-permute-done | bytes 262176 | tf_op jit(solution)/shard_map/ppermute | solution.py:36
  (204 shorter events, 81.8 us)
Async XLA Ops:
  2.8 11.8 %collective-permute-start.1 = (f32[24,128]{1,0:T(8,128)S(1)}, f32[24,128]{1,0:T(8,128)S(1)}, u32[]{:S(2)}, u32[]{:S(2)}) collective-permute-start(f32[24,128]{1,0:T(8,128)S(1)} %get-tuple-element.75), channel_id=1, source_target_pairs={{0,16},{1,17},{2,18},{3,19},{4,20},{5,21},{6,22},{7,23},{8,24},{9,... | collective-permute-start | bytes 36872 | tf_op jit(solution)/shard_map/ppermute | solution.py:36
  8.4 27.4 %collective-permute-start.4 = (bf16[128,1024]{1,0:T(8,128)(2,1)}, bf16[128,1024]{1,0:T(8,128)(2,1)S(1)}, u32[]{:S(2)}, u32[]{:S(2)}) collective-permute-start(bf16[128,1024]{1,0:T(8,128)(2,1)} %refs_0_.1), channel_id=1, source_target_pairs={{0,4},{1,5},{2,3},{3,2},{4,0},{5,1},{6,7},{7,6},{8,12},{9,13},{10,... | collective-permute-start | bytes 786440 | tf_op jit(solution)/shard_map/ppermute | solution.py:36
  9.9 20.3 %collective-permute-start.5 = (bf16[128,1024]{1,0:T(8,128)(2,1)}, bf16[128,1024]{1,0:T(8,128)(2,1)S(1)}, u32[]{:S(2)}, u32[]{:S(2)}) collective-permute-start(bf16[128,1024]{1,0:T(8,128)(2,1)} %refs_0_.1), channel_id=1, source_target_pairs={{0,8},{1,9},{2,10},{3,11},{4,12},{5,13},{6,14},{7,15},{8,0},{9,1},... | collective-permute-start | bytes 786440 | tf_op jit(solution)/shard_map/ppermute | solution.py:36
  10.4 16.2 %collective-permute-start.11 = (bf16[128,1024]{1,0:T(8,128)(2,1)}, bf16[128,1024]{1,0:T(8,128)(2,1)S(1)}, u32[]{:S(2)}, u32[]{:S(2)}) collective-permute-start(bf16[128,1024]{1,0:T(8,128)(2,1)} %refs_0_.1), channel_id=1, source_target_pairs={{0,16},{1,17},{2,18},{3,19},{4,20},{5,21},{6,22},{7,23},{8,24},{9,... | collective-permute-start | bytes 786440 | tf_op jit(solution)/shard_map/ppermute | solution.py:36
  28.4 15.3 %collective-permute-start.15 = (bf16[128,1024]{1,0:T(8,128)(2,1)S(1)}, bf16[128,1024]{1,0:T(8,128)(2,1)S(1)}, u32[]{:S(2)}, u32[]{:S(2)}) collective-permute-start(bf16[128,1024]{1,0:T(8,128)(2,1)S(1)} %copy-done.5), channel_id=1, source_target_pairs={{0,16},{1,17},{2,18},{3,19},{4,20},{5,21},{6,22},{7,23},{8,24},{9,... | collective-permute-start | bytes 786440 | tf_op jit(solution)/shard_map/ppermute | solution.py:36
  39.4 12.8 %collective-permute-start.7 = (bf16[2,2,48,1024]{3,2,1,0:T(8,128)(2,1)S(1)}, bf16[2,2,48,1024]{3,2,1,0:T(8,128)(2,1)S(1)}, u32[]{:S(2)}, u32[]{:S(2)}) collective-permute-start(bf16[2,2,48,1024]{3,2,1,0:T(8,128)(2,1)S(1)} %get-tuple-element.27), channel_id=1, source_target_pairs={{0,1},{1,0},{2,6},{3,7},{4,5},{5,4},{6,2},{7,3},{8,9},{9,8},{10,14... | collective-permute-start | bytes 1179656 | tf_op jit(solution)/shard_map/ppermute | solution.py:36
  40.1 12.1 %collective-permute-start.9 = (bf16[2,2,48,1024]{3,2,1,0:T(8,128)(2,1)S(1)}, bf16[2,2,48,1024]{3,2,1,0:T(8,128)(2,1)S(1)}, u32[]{:S(2)}, u32[]{:S(2)}) collective-permute-start(bf16[2,2,48,1024]{3,2,1,0:T(8,128)(2,1)S(1)} %get-tuple-element.29), channel_id=1, source_target_pairs={{0,1},{1,0},{2,6},{3,7},{4,5},{5,4},{6,2},{7,3},{8,9},{9,8},{10,14... | collective-permute-start | bytes 1179656 | tf_op jit(solution)/shard_map/ppermute | solution.py:36
  44.3 11.4 %collective-permute-start.18 = (bf16[2,2,48,1024]{3,2,1,0:T(8,128)(2,1)S(1)}, bf16[2,2,48,1024]{3,2,1,0:T(8,128)(2,1)S(1)}, u32[]{:S(2)}, u32[]{:S(2)}) collective-permute-start(bf16[2,2,48,1024]{3,2,1,0:T(8,128)(2,1)S(1)} %get-tuple-element.34), channel_id=1, source_target_pairs={{0,1},{1,0},{2,6},{3,7},{4,5},{5,4},{6,2},{7,3},{8,9},{9,8},{10,14... | collective-permute-start | bytes 1179656 | tf_op jit(solution)/shard_map/ppermute | solution.py:36
  56.1 14.9 %collective-permute-start.24 = (bf16[4,128,1024]{2,1,0:T(8,128)(2,1)S(1)}, bf16[4,128,1024]{2,1,0:T(8,128)(2,1)S(1)}, u32[]{:S(2)}, u32[]{:S(2)}) collective-permute-start(bf16[4,128,1024]{2,1,0:T(8,128)(2,1)S(1)} %pad_maximum_fusion.refs_0_), channel_id=1, source_target_pairs={{0,4},{1,5},{2,3},{3,2},{4,0},{5,1},{6,7},{7,6},{8,12},{9,13},{10,... | collective-permute-start | bytes 3145736 | tf_op jit(solution)/shard_map/ppermute | solution.py:36
  71.9 20.5 %collective-permute-start.28 = (bf16[2,2,4,48,1024]{4,3,2,1,0:T(8,128)(2,1)S(1)}, bf16[2,2,4,48,1024]{4,3,2,1,0:T(8,128)(2,1)S(1)}, u32[]{:S(2)}, u32[]{:S(2)}) collective-permute-start(bf16[2,2,4,48,1024]{4,3,2,1,0:T(8,128)(2,1)S(1)} %get-tuple-element.36), channel_id=1, source_target_pairs={{0,1},{1,0},{2,6},{3,7},{4,5},{5,4},{6,2},{7,3},{8,9},{9,8},{10,14... | collective-permute-start | bytes 4718600 | tf_op jit(solution)/shard_map/ppermute | solution.py:36
  81.3 11.4 %collective-permute-start.33 = (bf16[2,2,4,48,1024]{4,3,2,1,0:T(8,128)(2,1)S(1)}, bf16[2,2,4,48,1024]{4,3,2,1,0:T(8,128)(2,1)S(1)}, u32[]{:S(2)}, u32[]{:S(2)}) collective-permute-start(bf16[2,2,4,48,1024]{4,3,2,1,0:T(8,128)(2,1)S(1)} %slice_bitcast_fusion), channel_id=1, source_target_pairs={{0,2},{1,3},{2,0},{3,1},{4,6},{5,7},{6,4},{7,5},{8,10},{9,11},{10,... | collective-permute-start | bytes 4718600 | tf_op jit(solution)/shard_map/ppermute | solution.py:36
  81.7 11.7 %collective-permute-start.25 = (f32[4,2,2,4,128]{4,3,2,1,0:T(4,128)S(1)}, f32[4,2,2,4,128]{4,3,2,1,0:T(4,128)S(1)}, u32[]{:S(2)}, u32[]{:S(2)}) collective-permute-start(f32[4,2,2,4,128]{4,3,2,1,0:T(4,128)S(1)} %fusion.40), channel_id=1, source_target_pairs={{0,2},{1,3},{2,0},{3,1},{4,6},{5,7},{6,4},{7,5},{8,10},{9,11},{10,... | collective-permute-start | bytes 98312 | tf_op jit(solution)/shard_map/ppermute | solution.py:36
  82.2 20.4 %collective-permute-start.29 = (bf16[2,4,48,1024]{3,2,1,0:T(8,128)(2,1)S(1)}, bf16[2,4,48,1024]{3,2,1,0:T(8,128)(2,1)S(1)}, u32[]{:S(2)}, u32[]{:S(2)}) collective-permute-start(bf16[2,4,48,1024]{3,2,1,0:T(8,128)(2,1)S(1)} %get-tuple-element.64), channel_id=1, source_target_pairs={{0,2},{1,3},{2,0},{3,1},{4,6},{5,7},{6,4},{7,5},{8,10},{9,11},{10,... | collective-permute-start | bytes 2359304 | tf_op jit(solution)/shard_map/ppermute | solution.py:36
  82.6 25.6 %collective-permute-start.34 = (bf16[2,4,48,1024]{3,2,1,0:T(8,128)(2,1)S(1)}, bf16[2,4,48,1024]{3,2,1,0:T(8,128)(2,1)S(1)}, u32[]{:S(2)}, u32[]{:S(2)}) collective-permute-start(bf16[2,4,48,1024]{3,2,1,0:T(8,128)(2,1)S(1)} %slice_bitcast_fusion.2), channel_id=1, source_target_pairs={{0,1},{1,0},{2,6},{3,7},{4,5},{5,4},{6,2},{7,3},{8,9},{9,8},{10,14... | collective-permute-start | bytes 2359304 | tf_op jit(solution)/shard_map/ppermute | solution.py:36
  92.7 16.5 %collective-permute-start.35 = (bf16[2,4,48,1024]{3,2,1,0:T(8,128)(2,1)S(1)}, bf16[2,4,48,1024]{3,2,1,0:T(8,128)(2,1)S(1)}, u32[]{:S(2)}, u32[]{:S(2)}) collective-permute-start(bf16[2,4,48,1024]{3,2,1,0:T(8,128)(2,1)S(1)} %slice_bitcast_fusion.1), channel_id=1, source_target_pairs={{0,1},{1,0},{2,6},{3,7},{4,5},{5,4},{6,2},{7,3},{8,9},{9,8},{10,14... | collective-permute-start | bytes 2359304 | tf_op jit(solution)/shard_map/ppermute | solution.py:36
  110.9 19.2 %collective-permute-start.36 = (bf16[4,128,1024]{2,1,0:T(8,128)(2,1)S(1)}, bf16[4,128,1024]{2,1,0:T(8,128)(2,1)S(1)}, u32[]{:S(2)}, u32[]{:S(2)}) collective-permute-start(bf16[4,128,1024]{2,1,0:T(8,128)(2,1)S(1)} %get-tuple-element.39), channel_id=1, source_target_pairs={{0,4},{1,5},{2,3},{3,2},{4,0},{5,1},{6,7},{7,6},{8,12},{9,13},{10,... | collective-permute-start | bytes 3145736 | tf_op jit(solution)/shard_map/ppermute | solution.py:36
  128.3 15.5 %collective-permute-start.40 = (bf16[2,2,2,48,1024]{4,3,2,1,0:T(8,128)(2,1)S(1)}, bf16[2,2,2,48,1024]{4,3,2,1,0:T(8,128)(2,1)S(1)}, u32[]{:S(2)}, u32[]{:S(2)}) collective-permute-start(bf16[2,2,2,48,1024]{4,3,2,1,0:T(8,128)(2,1)S(1)} %slice_bitcast_fusion.6), channel_id=1, source_target_pairs={{0,2},{1,3},{2,0},{3,1},{4,6},{5,7},{6,4},{7,5},{8,10},{9,11},{10,... | collective-permute-start | bytes 2359304 | tf_op jit(solution)/shard_map/ppermute | solution.py:36
  135.5 12.1 %collective-permute-start.37 = (bf16[128,1024]{1,0:T(8,128)(2,1)S(1)}, bf16[128,1024]{1,0:T(8,128)(2,1)S(1)}, u32[]{:S(2)}, u32[]{:S(2)}) collective-permute-start(bf16[128,1024]{1,0:T(8,128)(2,1)S(1)} %get-tuple-element.66), channel_id=1, source_target_pairs={{0,8},{1,9},{2,10},{3,11},{4,12},{5,13},{6,14},{7,15},{8,0},{9,1},... | collective-permute-start | bytes 786440 | tf_op jit(solution)/shard_map/ppermute | solution.py:36
  140.4 15.4 %collective-permute-start.46 = (bf16[2,128,1024]{2,1,0:T(8,128)(2,1)S(1)}, bf16[2,128,1024]{2,1,0:T(8,128)(2,1)S(1)}, u32[]{:S(2)}, u32[]{:S(2)}) collective-permute-start(bf16[2,128,1024]{2,1,0:T(8,128)(2,1)S(1)} %get-tuple-element.43), channel_id=1, source_target_pairs={{0,4},{1,5},{2,3},{3,2},{4,0},{5,1},{6,7},{7,6},{8,12},{9,13},{10,... | collective-permute-start | bytes 1572872 | tf_op jit(solution)/shard_map/ppermute | solution.py:36
  141.6 13.3 %collective-permute-start.39 = (bf16[128,1024]{1,0:T(8,128)(2,1)S(1)}, bf16[128,1024]{1,0:T(8,128)(2,1)S(1)}, u32[]{:S(2)}, u32[]{:S(2)}) collective-permute-start(bf16[128,1024]{1,0:T(8,128)(2,1)S(1)} %fusion.13), channel_id=1, source_target_pairs={{0,16},{1,17},{2,18},{3,19},{4,20},{5,21},{6,22},{7,23},{8,24},{9,... | collective-permute-start | bytes 786440 | tf_op jit(solution)/shard_map/ppermute | solution.py:36
  143.5 12.8 %collective-permute-start.41 = (bf16[2,2,48,1024]{3,2,1,0:T(8,128)(2,1)S(1)}, bf16[2,2,48,1024]{3,2,1,0:T(8,128)(2,1)S(1)}, u32[]{:S(2)}, u32[]{:S(2)}) collective-permute-start(bf16[2,2,48,1024]{3,2,1,0:T(8,128)(2,1)S(1)} %slice_bitcast_fusion.16), channel_id=1, source_target_pairs={{0,1},{1,0},{2,6},{3,7},{4,5},{5,4},{6,2},{7,3},{8,9},{9,8},{10,14... | collective-permute-start | bytes 1179656 | tf_op jit(solution)/shard_map/ppermute | solution.py:36
  143.9 12.5 %collective-permute-start.42 = (bf16[2,2,48,1024]{3,2,1,0:T(8,128)(2,1)S(1)}, bf16[2,2,48,1024]{3,2,1,0:T(8,128)(2,1)S(1)}, u32[]{:S(2)}, u32[]{:S(2)}) collective-permute-start(bf16[2,2,48,1024]{3,2,1,0:T(8,128)(2,1)S(1)} %slice_bitcast_fusion.14), channel_id=1, source_target_pairs={{0,1},{1,0},{2,6},{3,7},{4,5},{5,4},{6,2},{7,3},{8,9},{9,8},{10,14... | collective-permute-start | bytes 1179656 | tf_op jit(solution)/shard_map/ppermute | solution.py:36
  162.6 15.6 %collective-permute-start.50 = (bf16[128,1024]{1,0:T(8,128)(2,1)S(1)}, bf16[128,1024]{1,0:T(8,128)(2,1)S(1)}, u32[]{:S(2)}, u32[]{:S(2)}) collective-permute-start(bf16[128,1024]{1,0:T(8,128)(2,1)S(1)} %fusion.8), channel_id=1, source_target_pairs={{0,16},{1,17},{2,18},{3,19},{4,20},{5,21},{6,22},{7,23},{8,24},{9,... | collective-permute-start | bytes 786440 | tf_op jit(solution)/shard_map/ppermute | solution.py:36
  166.7 14.0 %collective-permute-start.48 = (bf16[128,1024]{1,0:T(8,128)(2,1)S(1)}, bf16[128,1024]{1,0:T(8,128)(2,1)S(1)}, u32[]{:S(2)}, u32[]{:S(2)}) collective-permute-start(bf16[128,1024]{1,0:T(8,128)(2,1)S(1)} %fusion.16), channel_id=1, source_target_pairs={{0,8},{1,9},{2,10},{3,11},{4,12},{5,13},{6,14},{7,15},{8,0},{9,1},... | collective-permute-start | bytes 786440 | tf_op jit(solution)/shard_map/ppermute | solution.py:36
  (37 other events, 344.3 us)

commit v3 on v2

--- a/solution.py
+++ b/solution.py
@@ -390,10 +390,10 @@
 
 def gather_by_column(column, after, pos, groups, n, cap):
     units = [[value] + [send_first(value, k) for k in range(1, n)] for value in column]
-    routed = [
-        route_rows([units[k] for k in members], more, pos, members[0], cap)
-        for members, more in zip(groups, after)
-    ]
+    routed = []
+    for members, more in zip(groups, after):
+        more = more + [rows[0] for _, rows in routed]
+        routed.append(route_rows([units[k] for k in members], more, pos, members[0], cap))
     return [pieces for pieces, _ in routed], routed[0][1]
 
 
@@ -557,7 +557,7 @@
 
     later_in = lax.optimization_barrier([grad_later, hidden_column[depth // 2]])[0]
     later_column = z_gather(later_in, depth, n)
-    pieces, _ = gather_by_column(hidden_column, [[], later_column[depth // 2 : depth // 2 + 1]], pos, two, n, cap)
+    pieces, _ = gather_by_column(hidden_column, [[down_head], later_column[depth // 2 : depth // 2 + 1]], pos, two, n, cap)
 
     def normed(out_ref, features_ref):
         for b in range(2 * n):

time: 186 us -> 186 us (level)
  transfers between devices with their start and end apart: 52 -> 52, of which waited for: 24 -> 25; matrix products, arithmetic and copies ran while one was open for 17% -> 17% of each run, Pallas kernels for 14% -> 14%
where the time goes in v3:
time: 186 us
  waiting for transfers between devices  71.3 us (38%)
  starting transfers between devices  49.4 us (27%)
  Pallas kernels  27.9 us (15%)
  matrix products  26.3 us (14%)
  other arithmetic  8.31 us (4%)
    ppermute x52, waiting for transfers between devices, send(): return lax.ppermute(value, ('ep', 'tp'), pairs)  71.3 us
    ppermute x52, starting transfers between devices, send(): return lax.ppermute(value, ('ep', 'tp'), pairs)  49.4 us
    pallas_call x2, Pallas kernels, column_product(): pl.pallas_call(body, grid_spec=pltpu.PrefetchScalarGridSpec(num_scalar_pr...  14.7 us
    dot_general x3, matrix products, over_rows(): lax.dot_general(left, right, (((0,), (0,)), ((), ())), preferred_element_...  12 us
    dot_general x3, matrix products, against(): lax.dot_general(left, right, (((1,), (1,)), ((), ())), preferred_element_...  8.74 us
    pallas_call x2, Pallas kernels, assemble(): pl.pallas_call(body, grid_spec=pltpu.PrefetchScalarGridSpec(num_scalar_pr...  5.96 us
  transfers between devices with their start and end apart: 52, of which 25 were waited for; matrix products, arithmetic and copies ran while one was open for 17% of the time, Pallas kernels for 14%

profile of v3, /device:TPU:0, one launch (start us, length us, event | category | flops | bytes accessed | tf_op | source)
XLA Modules:
  0.0 185.8 jit_solution(5804871621575359986)
XLA Ops:
  2.8 4.0 %collective-permute-start.1 = (f32[24,128]{1,0:T(8,128)S(1)}, f32[24,128]{1,0:T(8,128)S(1)}, u32[]{:S(2)}, u32[]{:S(2)}) collective-permute-start(f32[24,128]{1,0:T(8,128)S(1)} %get-tuple-element.75), channel_id=1, source_target_pairs={{0,16},{1,17},{2,18},{3,19},{4,20},{5,21},{6,22},{7,23},{8,24},{9,... | collective-permute-start | bytes 36872 | tf_op jit(solution)/shard_map/ppermute | solution.py:36
  18.0 4.1 %collective-permute-done.2 = f32[24,128]{1,0:T(8,128)S(1)} collective-permute-done((f32[24,128]{1,0:T(8,128)S(1)}, f32[24,128]{1,0:T(8,128)S(1)}, u32[]{:S(2)}, u32[]{:S(2)}) %collective-permute-start.2) | collective-permute-done | bytes 12320 | tf_op jit(solution)/shard_map/ppermute | solution.py:36
  23.7 2.8 %fusion.35.refs_4_.head_ref = bf16[16,768]{1,0:T(8,128)(2,1)S(1)} fusion(bf16[768,2048]{1,0:T(8,128)(2,1)} %refs_1_.2, bf16[4,2048]{1,0:T(4,128)(2,1)S(1)} %bitcast.197, bf16[4,2048]{1,0:T(4,128)(2,1)S(1)} %broadcast_in_dim.65, pred[16]{0:T(512)(128)(4,1)S(1)} %iota_compare_fusion.5), kind=kOutput, calls=%fused_computation.98 | convolution fusion | flops 50655232 | bytes 3203088 | tf_op jit(solution)/shard_map/dot_general | solution.py:551
  31.7 3.4 %collective-permute-done.14.refs_2_ = bf16[128,1024]{1,0:T(8,128)(2,1)S(1)} collective-permute-done((bf16[128,1024]{1,0:T(8,128)(2,1)S(1)}, bf16[128,1024]{1,0:T(8,128)(2,1)S(1)}, u32[]{:S(2)}, u32[]{:S(2)}) %collective-permute-start.14) | collective-permute-done | bytes 262176 | tf_op jit(solution)/shard_map/ppermute | solution.py:36
  45.1 6.5 %collective-permute-done.23 = bf16[128,1024]{1,0:T(8,128)(2,1)S(1)} collective-permute-done((bf16[128,1024]{1,0:T(8,128)(2,1)S(1)}, bf16[128,1024]{1,0:T(8,128)(2,1)S(1)}, u32[]{:S(2)}, u32[]{:S(2)}) %collective-permute-start.23) | collective-permute-done | bytes 262176 | tf_op jit(solution)/shard_map/ppermute | solution.py:36
  52.7 3.0 %collective-permute-done.19 = bf16[2,2,48,1024]{3,2,1,0:T(8,128)(2,1)S(1)} collective-permute-done((bf16[2,2,48,1024]{3,2,1,0:T(8,128)(2,1)S(1)}, bf16[2,2,48,1024]{3,2,1,0:T(8,128)(2,1)S(1)}, u32[]{:S(2)}, u32[]{:S(2)}) %collective-permute-start.19) | collective-permute-done | bytes 393248 | tf_op jit(solution)/shard_map/ppermute | solution.py:36
  57.2 3.3 %collective-permute-done.17.refs_5_ = bf16[2,2,48,1024]{3,2,1,0:T(8,128)(2,1)S(1)} collective-permute-done((bf16[2,2,48,1024]{3,2,1,0:T(8,128)(2,1)S(1)}, bf16[2,2,48,1024]{3,2,1,0:T(8,128)(2,1)S(1)}, u32[]{:S(2)}, u32[]{:S(2)}) %collective-permute-start.17) | collective-permute-done | bytes 393248 | tf_op jit(solution)/shard_map/ppermute | solution.py:36
  60.5 2.7 %normed_rows.1 = bf16[4,4,48,2048]{3,2,1,0:T(8,128)(2,1)S(1)} custom-call(s32[2]{0:T(128)S(1)} %pad_add_fusion.place_ref, bf16[2,2,48,1024]{3,2,1,0:T(8,128)(2,1)S(1)} %get-tuple-element.26.refs_5_.refs_0_, bf16[2,2,48,1024]{3,2,1,0:T(8,128)(2,1)S(1)} %collective-permute-done.8.refs_1_, bf16[2,2,48,1024]{3,2,1,0:T(8,128)(2,1)S(1)} %collective-permute-done.9.refs_2_, ...), custom_call_target="tpu_custom_call" | custom-call | flops 15728640 | bytes 6291456 | tf_op jit(solution)/shard_map/normed_rows/pallas_call | solution.py:223
  63.2 2.6 %fusion.76 = f32[768,768]{1,0:T(8,128)S(1)} fusion(bf16[768,2048]{1,0:T(8,128)(2,1)S(1)} %bitcast.176, bf16[768,2048]{1,0:T(8,128)(2,1)S(1)} %copy-done.3), kind=kOutput, calls=%fused_computation.166 | convolution fusion | flops 2415919104 | bytes 8650752 | tf_op jit(solution)/shard_map/dot_general | solution.py:582
  65.8 2.8 %multiply_convert_fusion.2 = (bf16[768,768]{1,0:T(8,128)(2,1)S(1)}, f32[768,768]{1,0:T(8,128)S(1)}) fusion(f32[768,768]{1,0:T(8,128)S(1)} %fusion.76, bf16[768,2048]{1,0:T(8,128)(2,1)S(1)} %bitcast.177, bf16[768,2048]{1,0:T(8,128)(2,1)S(1)} %copy-done.4), kind=kOutput, calls=%fused_computation.5 | convolution fusion | flops 2419458048 | bytes 12189696 | tf_op jit(solution)/shard_map/dot_general | solution.py:582
  74.5 6.6 %out_rows.1.refs_1_ = bf16[2,2,2,4,48,1024]{5,4,3,2,1,0:T(8,128)(2,1)S(1)} custom-call(s32[2]{0:T(128)S(1)} %pad_add_fusion.place_ref, bf16[4,4,48,768]{3,2,1,0:T(8,128)(2,1)S(1)} %bitcast.175, bf16[768,2048]{1,0:T(8,128)(2,1)S(1)} %copy-done, f32[4,4,1,128]{3,2,1,0:T(1,128)S(1)} %bitcast.188, bf16[4,4,16,128]{3,2,1,0:T(8,128)(2,1)S(1)} %maximum_maximum_fusion.refs_3_, ...), custom_call_target="tpu_custom_call" | custom-call | flops 2415919104 | bytes 7471104 | tf_op jit(solution)/shard_map/out_rows/pallas_call | solution.py:285
  83.8 8.5 %collective-permute-done.28 = bf16[2,2,4,48,1024]{4,3,2,1,0:T(8,128)(2,1)S(1)} collective-permute-done((bf16[2,2,4,48,1024]{4,3,2,1,0:T(8,128)(2,1)S(1)}, bf16[2,2,4,48,1024]{4,3,2,1,0:T(8,128)(2,1)S(1)}, u32[]{:S(2)}, u32[]{:S(2)}) %collective-permute-start.28) | collective-permute-done | bytes 1572896 | tf_op jit(solution)/shard_map/ppermute | solution.py:36
  94.3 3.0 %collective-permute-done.26 = f32[4,2,2,4,128]{4,3,2,1,0:T(4,128)S(1)} collective-permute-done((f32[4,2,2,4,128]{4,3,2,1,0:T(4,128)S(1)}, f32[4,2,2,4,128]{4,3,2,1,0:T(4,128)S(1)}, u32[]{:S(2)}, u32[]{:S(2)}) %collective-permute-start.26) | collective-permute-done | bytes 32800 | tf_op jit(solution)/shard_map/ppermute | solution.py:36
  99.3 3.3 %collective-permute-done.27 = f32[4,2,2,4,128]{4,3,2,1,0:T(4,128)S(1)} collective-permute-done((f32[4,2,2,4,128]{4,3,2,1,0:T(4,128)S(1)}, f32[4,2,2,4,128]{4,3,2,1,0:T(4,128)S(1)}, u32[]{:S(2)}, u32[]{:S(2)}) %collective-permute-start.27) | collective-permute-done | bytes 32800 | tf_op jit(solution)/shard_map/ppermute | solution.py:36
  103.5 3.5 %collective-permute-done.31 = f32[4,2,2,4,128]{4,3,2,1,0:T(4,128)S(1)} collective-permute-done((f32[4,2,2,4,128]{4,3,2,1,0:T(4,128)S(1)}, f32[4,2,2,4,128]{4,3,2,1,0:T(4,128)S(1)}, u32[]{:S(2)}, u32[]{:S(2)}) %collective-permute-start.31) | collective-permute-done | bytes 32800 | tf_op jit(solution)/shard_map/ppermute | solution.py:36
  112.2 3.3 %gradient_rows.1 = bf16[4,4,48,2048]{3,2,1,0:T(8,128)(2,1)S(1)} custom-call(s32[2]{0:T(128)S(1)} %pad_add_fusion.place_ref, bf16[2,4,48,1024]{3,2,1,0:T(8,128)(2,1)S(1)} %get-tuple-element.65.refs_0_, bf16[2,4,48,1024]{3,2,1,0:T(8,128)(2,1)S(1)} %get-tuple-element.63.refs_1_, bf16[2,4,48,1024]{3,2,1,0:T(8,128)(2,1)S(1)} %collective-permute-done.29.refs_2_, ...), custom_call_target="tpu_custom_call" | custom-call | flops 15728640 | bytes 6291456 | tf_op jit(solution)/shard_map/gradient_rows/pallas_call | solution.py:223
  115.5 3.3 %multiply_convert_fusion = (bf16[768,768]{1,0:T(8,128)(2,1)S(1)}, bf16[768,768]{1,0:T(8,128)(2,1)S(1)}) fusion(f32[768,768]{1,0:T(8,128)S(1)} %fusion.76, f32[768,768]{1,0:T(8,128)S(1)} %get-tuple-element.81, bf16[768,2048]{1,0:T(8,128)(2,1)S(1)} %bitcast.180, bf16[768,2048]{1,0:T(8,128)(2,1)S(1)} %copy-done), kind=kOutput, calls=%fused_computation.3 | convolution fusion | flops 2423586816 | bytes 13369344 | tf_op jit(solution)/shard_map/dot_general | solution.py:582
  118.8 8.0 %d_rows.1 = (bf16[2,2,2,2,48,1024]{5,4,3,2,1,0:T(8,128)(2,1)S(1)}, bf16[2,2,2,2,48,1024]{5,4,3,2,1,0:T(8,128)(2,1)S(1)}) custom-call(s32[2]{0:T(128)S(1)} %pad_add_fusion.place_ref, bf16[4,4,48,768]{3,2,1,0:T(8,128)(2,1)S(1)} %bitcast.191, bf16[768,2048]{1,0:T(8,128)(2,1)S(1)} %copy-done.3, bf16[4,4,48,768]{3,2,1,0:T(8,128)(2,1)S(1)} %bitcast.190, ...), custom_call_target="tpu_custom_call" | custom-call | flops 4831838208 | bytes 11796480 | tf_op jit(solution)/shard_map/d_rows/pallas_call | solution.py:285
  131.5 4.0 %convolution_convert_fusion.2 = bf16[768,2048]{1,0:T(8,128)(2,1)} fusion(bf16[768,768]{1,0:T(8,128)(2,1)S(1)} %get-tuple-element.59, bf16[768,2048]{1,0:T(8,128)(2,1)S(1)} %bitcast.178), kind=kOutput, calls=%fused_computation.2 | convolution fusion | flops 2417491968 | bytes 7471104 | tf_op jit(solution)/shard_map/dot_general | solution.py:585
  136.7 2.9 %collective-permute-done.45.refs_4_ = bf16[2,2,48,1024]{3,2,1,0:T(8,128)(2,1)S(1)} collective-permute-done((bf16[2,2,48,1024]{3,2,1,0:T(8,128)(2,1)S(1)}, bf16[2,2,48,1024]{3,2,1,0:T(8,128)(2,1)S(1)}, u32[]{:S(2)}, u32[]{:S(2)}) %collective-permute-start.45) | collective-permute-done | bytes 393248 | tf_op jit(solution)/shard_map/ppermute | solution.py:36
  147.6 7.3 %collective-permute-done.39 = bf16[128,1024]{1,0:T(8,128)(2,1)S(1)} collective-permute-done((bf16[128,1024]{1,0:T(8,128)(2,1)S(1)}, bf16[128,1024]{1,0:T(8,128)(2,1)S(1)}, u32[]{:S(2)}, u32[]{:S(2)}) %collective-permute-start.39) | collective-permute-done | bytes 262176 | tf_op jit(solution)/shard_map/ppermute | solution.py:36
  158.3 4.0 %convolution_convert_fusion.1 = bf16[768,2048]{1,0:T(8,128)(2,1)} fusion(bf16[768,768]{1,0:T(8,128)(2,1)S(1)} %get-tuple-element.58, bf16[768,2048]{1,0:T(8,128)(2,1)S(1)} %bitcast.179), kind=kOutput, calls=%fused_computation.1 | convolution fusion | flops 2417491968 | bytes 7471104 | tf_op jit(solution)/shard_map/dot_general | solution.py:585
  168.6 4.0 %convolution_convert_fusion = bf16[768,2048]{1,0:T(8,128)(2,1)} fusion(bf16[768,768]{1,0:T(8,128)(2,1)S(1)} %get-tuple-element.80, bf16[768,2048]{1,0:T(8,128)(2,1)S(1)} %bitcast.181), kind=kOutput, calls=%fused_computation | convolution fusion | flops 2417491968 | bytes 7471104 | tf_op jit(solution)/shard_map/dot_general | solution.py:585
  172.6 5.6 %collective-permute-done.50 = bf16[128,1024]{1,0:T(8,128)(2,1)S(1)} collective-permute-done((bf16[128,1024]{1,0:T(8,128)(2,1)S(1)}, bf16[128,1024]{1,0:T(8,128)(2,1)S(1)}, u32[]{:S(2)}, u32[]{:S(2)}) %collective-permute-start.50) | collective-permute-done | bytes 262176 | tf_op jit(solution)/shard_map/ppermute | solution.py:36
  (204 shorter events, 81.8 us)
Async XLA Ops:
  2.8 11.8 %collective-permute-start.1 = (f32[24,128]{1,0:T(8,128)S(1)}, f32[24,128]{1,0:T(8,128)S(1)}, u32[]{:S(2)}, u32[]{:S(2)}) collective-permute-start(f32[24,128]{1,0:T(8,128)S(1)} %get-tuple-element.75), channel_id=1, source_target_pairs={{0,16},{1,17},{2,18},{3,19},{4,20},{5,21},{6,22},{7,23},{8,24},{9,... | collective-permute-start | bytes 36872 | tf_op jit(solution)/shard_map/ppermute | solution.py:36
  8.4 27.4 %collective-permute-start.4 = (bf16[128,1024]{1,0:T(8,128)(2,1)}, bf16[128,1024]{1,0:T(8,128)(2,1)S(1)}, u32[]{:S(2)}, u32[]{:S(2)}) collective-permute-start(bf16[128,1024]{1,0:T(8,128)(2,1)} %refs_0_.1), channel_id=1, source_target_pairs={{0,4},{1,5},{2,3},{3,2},{4,0},{5,1},{6,7},{7,6},{8,12},{9,13},{10,... | collective-permute-start | bytes 786440 | tf_op jit(solution)/shard_map/ppermute | solution.py:36
  9.9 20.3 %collective-permute-start.5 = (bf16[128,1024]{1,0:T(8,128)(2,1)}, bf16[128,1024]{1,0:T(8,128)(2,1)S(1)}, u32[]{:S(2)}, u32[]{:S(2)}) collective-permute-start(bf16[128,1024]{1,0:T(8,128)(2,1)} %refs_0_.1), channel_id=1, source_target_pairs={{0,8},{1,9},{2,10},{3,11},{4,12},{5,13},{6,14},{7,15},{8,0},{9,1},... | collective-permute-start | bytes 786440 | tf_op jit(solution)/shard_map/ppermute | solution.py:36
  10.4 16.2 %collective-permute-start.12 = (bf16[128,1024]{1,0:T(8,128)(2,1)}, bf16[128,1024]{1,0:T(8,128)(2,1)S(1)}, u32[]{:S(2)}, u32[]{:S(2)}) collective-permute-start(bf16[128,1024]{1,0:T(8,128)(2,1)} %refs_0_.1), channel_id=1, source_target_pairs={{0,16},{1,17},{2,18},{3,19},{4,20},{5,21},{6,22},{7,23},{8,24},{9,... | collective-permute-start | bytes 786440 | tf_op jit(solution)/shard_map/ppermute | solution.py:36
  28.4 15.3 %collective-permute-start.16 = (bf16[128,1024]{1,0:T(8,128)(2,1)S(1)}, bf16[128,1024]{1,0:T(8,128)(2,1)S(1)}, u32[]{:S(2)}, u32[]{:S(2)}) collective-permute-start(bf16[128,1024]{1,0:T(8,128)(2,1)S(1)} %copy-done.5), channel_id=1, source_target_pairs={{0,16},{1,17},{2,18},{3,19},{4,20},{5,21},{6,22},{7,23},{8,24},{9,... | collective-permute-start | bytes 786440 | tf_op jit(solution)/shard_map/ppermute | solution.py:36
  39.4 12.8 %collective-permute-start.8 = (bf16[2,2,48,1024]{3,2,1,0:T(8,128)(2,1)S(1)}, bf16[2,2,48,1024]{3,2,1,0:T(8,128)(2,1)S(1)}, u32[]{:S(2)}, u32[]{:S(2)}) collective-permute-start(bf16[2,2,48,1024]{3,2,1,0:T(8,128)(2,1)S(1)} %get-tuple-element.27), channel_id=1, source_target_pairs={{0,1},{1,0},{2,6},{3,7},{4,5},{5,4},{6,2},{7,3},{8,9},{9,8},{10,14... | collective-permute-start | bytes 1179656 | tf_op jit(solution)/shard_map/ppermute | solution.py:36
  40.1 12.1 %collective-permute-start.10 = (bf16[2,2,48,1024]{3,2,1,0:T(8,128)(2,1)S(1)}, bf16[2,2,48,1024]{3,2,1,0:T(8,128)(2,1)S(1)}, u32[]{:S(2)}, u32[]{:S(2)}) collective-permute-start(bf16[2,2,48,1024]{3,2,1,0:T(8,128)(2,1)S(1)} %get-tuple-element.29), channel_id=1, source_target_pairs={{0,1},{1,0},{2,6},{3,7},{4,5},{5,4},{6,2},{7,3},{8,9},{9,8},{10,14... | collective-permute-start | bytes 1179656 | tf_op jit(solution)/shard_map/ppermute | solution.py:36
  44.3 11.4 %collective-permute-start.19 = (bf16[2,2,48,1024]{3,2,1,0:T(8,128)(2,1)S(1)}, bf16[2,2,48,1024]{3,2,1,0:T(8,128)(2,1)S(1)}, u32[]{:S(2)}, u32[]{:S(2)}) collective-permute-start(bf16[2,2,48,1024]{3,2,1,0:T(8,128)(2,1)S(1)} %get-tuple-element.34), channel_id=1, source_target_pairs={{0,1},{1,0},{2,6},{3,7},{4,5},{5,4},{6,2},{7,3},{8,9},{9,8},{10,14... | collective-permute-start | bytes 1179656 | tf_op jit(solution)/shard_map/ppermute | solution.py:36
  56.1 14.9 %collective-permute-start.24 = (bf16[4,128,1024]{2,1,0:T(8,128)(2,1)S(1)}, bf16[4,128,1024]{2,1,0:T(8,128)(2,1)S(1)}, u32[]{:S(2)}, u32[]{:S(2)}) collective-permute-start(bf16[4,128,1024]{2,1,0:T(8,128)(2,1)S(1)} %pad_maximum_fusion.refs_0_), channel_id=1, source_target_pairs={{0,4},{1,5},{2,3},{3,2},{4,0},{5,1},{6,7},{7,6},{8,12},{9,13},{10,... | collective-permute-start | bytes 3145736 | tf_op jit(solution)/shard_map/ppermute | solution.py:36
  71.9 20.5 %collective-permute-start.28 = (bf16[2,2,4,48,1024]{4,3,2,1,0:T(8,128)(2,1)S(1)}, bf16[2,2,4,48,1024]{4,3,2,1,0:T(8,128)(2,1)S(1)}, u32[]{:S(2)}, u32[]{:S(2)}) collective-permute-start(bf16[2,2,4,48,1024]{4,3,2,1,0:T(8,128)(2,1)S(1)} %get-tuple-element.36), channel_id=1, source_target_pairs={{0,1},{1,0},{2,6},{3,7},{4,5},{5,4},{6,2},{7,3},{8,9},{9,8},{10,14... | collective-permute-start | bytes 4718600 | tf_op jit(solution)/shard_map/ppermute | solution.py:36
  81.3 11.4 %collective-permute-start.33 = (bf16[2,2,4,48,1024]{4,3,2,1,0:T(8,128)(2,1)S(1)}, bf16[2,2,4,48,1024]{4,3,2,1,0:T(8,128)(2,1)S(1)}, u32[]{:S(2)}, u32[]{:S(2)}) collective-permute-start(bf16[2,2,4,48,1024]{4,3,2,1,0:T(8,128)(2,1)S(1)} %slice_bitcast_fusion), channel_id=1, source_target_pairs={{0,2},{1,3},{2,0},{3,1},{4,6},{5,7},{6,4},{7,5},{8,10},{9,11},{10,... | collective-permute-start | bytes 4718600 | tf_op jit(solution)/shard_map/ppermute | solution.py:36
  81.8 11.6 %collective-permute-start.25 = (f32[4,2,2,4,128]{4,3,2,1,0:T(4,128)S(1)}, f32[4,2,2,4,128]{4,3,2,1,0:T(4,128)S(1)}, u32[]{:S(2)}, u32[]{:S(2)}) collective-permute-start(f32[4,2,2,4,128]{4,3,2,1,0:T(4,128)S(1)} %fusion.40), channel_id=1, source_target_pairs={{0,2},{1,3},{2,0},{3,1},{4,6},{5,7},{6,4},{7,5},{8,10},{9,11},{10,... | collective-permute-start | bytes 98312 | tf_op jit(solution)/shard_map/ppermute | solution.py:36
  82.2 20.4 %collective-permute-start.29 = (bf16[2,4,48,1024]{3,2,1,0:T(8,128)(2,1)S(1)}, bf16[2,4,48,1024]{3,2,1,0:T(8,128)(2,1)S(1)}, u32[]{:S(2)}, u32[]{:S(2)}) collective-permute-start(bf16[2,4,48,1024]{3,2,1,0:T(8,128)(2,1)S(1)} %get-tuple-element.64), channel_id=1, source_target_pairs={{0,2},{1,3},{2,0},{3,1},{4,6},{5,7},{6,4},{7,5},{8,10},{9,11},{10,... | collective-permute-start | bytes 2359304 | tf_op jit(solution)/shard_map/ppermute | solution.py:36
  82.6 25.6 %collective-permute-start.34 = (bf16[2,4,48,1024]{3,2,1,0:T(8,128)(2,1)S(1)}, bf16[2,4,48,1024]{3,2,1,0:T(8,128)(2,1)S(1)}, u32[]{:S(2)}, u32[]{:S(2)}) collective-permute-start(bf16[2,4,48,1024]{3,2,1,0:T(8,128)(2,1)S(1)} %slice_bitcast_fusion.2), channel_id=1, source_target_pairs={{0,1},{1,0},{2,6},{3,7},{4,5},{5,4},{6,2},{7,3},{8,9},{9,8},{10,14... | collective-permute-start | bytes 2359304 | tf_op jit(solution)/shard_map/ppermute | solution.py:36
  92.7 16.5 %collective-permute-start.35 = (bf16[2,4,48,1024]{3,2,1,0:T(8,128)(2,1)S(1)}, bf16[2,4,48,1024]{3,2,1,0:T(8,128)(2,1)S(1)}, u32[]{:S(2)}, u32[]{:S(2)}) collective-permute-start(bf16[2,4,48,1024]{3,2,1,0:T(8,128)(2,1)S(1)} %slice_bitcast_fusion.1), channel_id=1, source_target_pairs={{0,1},{1,0},{2,6},{3,7},{4,5},{5,4},{6,2},{7,3},{8,9},{9,8},{10,14... | collective-permute-start | bytes 2359304 | tf_op jit(solution)/shard_map/ppermute | solution.py:36
  110.9 19.2 %collective-permute-start.36 = (bf16[4,128,1024]{2,1,0:T(8,128)(2,1)S(1)}, bf16[4,128,1024]{2,1,0:T(8,128)(2,1)S(1)}, u32[]{:S(2)}, u32[]{:S(2)}) collective-permute-start(bf16[4,128,1024]{2,1,0:T(8,128)(2,1)S(1)} %get-tuple-element.39), channel_id=1, source_target_pairs={{0,4},{1,5},{2,3},{3,2},{4,0},{5,1},{6,7},{7,6},{8,12},{9,13},{10,... | collective-permute-start | bytes 3145736 | tf_op jit(solution)/shard_map/ppermute | solution.py:36
  128.3 15.5 %collective-permute-start.40 = (bf16[2,2,2,48,1024]{4,3,2,1,0:T(8,128)(2,1)S(1)}, bf16[2,2,2,48,1024]{4,3,2,1,0:T(8,128)(2,1)S(1)}, u32[]{:S(2)}, u32[]{:S(2)}) collective-permute-start(bf16[2,2,2,48,1024]{4,3,2,1,0:T(8,128)(2,1)S(1)} %slice_bitcast_fusion.6), channel_id=1, source_target_pairs={{0,2},{1,3},{2,0},{3,1},{4,6},{5,7},{6,4},{7,5},{8,10},{9,11},{10,... | collective-permute-start | bytes 2359304 | tf_op jit(solution)/shard_map/ppermute | solution.py:36
  135.5 12.2 %collective-permute-start.37 = (bf16[128,1024]{1,0:T(8,128)(2,1)S(1)}, bf16[128,1024]{1,0:T(8,128)(2,1)S(1)}, u32[]{:S(2)}, u32[]{:S(2)}) collective-permute-start(bf16[128,1024]{1,0:T(8,128)(2,1)S(1)} %get-tuple-element.66), channel_id=1, source_target_pairs={{0,8},{1,9},{2,10},{3,11},{4,12},{5,13},{6,14},{7,15},{8,0},{9,1},... | collective-permute-start | bytes 786440 | tf_op jit(solution)/shard_map/ppermute | solution.py:36
  140.4 15.4 %collective-permute-start.46 = (bf16[2,128,1024]{2,1,0:T(8,128)(2,1)S(1)}, bf16[2,128,1024]{2,1,0:T(8,128)(2,1)S(1)}, u32[]{:S(2)}, u32[]{:S(2)}) collective-permute-start(bf16[2,128,1024]{2,1,0:T(8,128)(2,1)S(1)} %get-tuple-element.43), channel_id=1, source_target_pairs={{0,4},{1,5},{2,3},{3,2},{4,0},{5,1},{6,7},{7,6},{8,12},{9,13},{10,... | collective-permute-start | bytes 1572872 | tf_op jit(solution)/shard_map/ppermute | solution.py:36
  141.6 13.3 %collective-permute-start.39 = (bf16[128,1024]{1,0:T(8,128)(2,1)S(1)}, bf16[128,1024]{1,0:T(8,128)(2,1)S(1)}, u32[]{:S(2)}, u32[]{:S(2)}) collective-permute-start(bf16[128,1024]{1,0:T(8,128)(2,1)S(1)} %fusion.13), channel_id=1, source_target_pairs={{0,16},{1,17},{2,18},{3,19},{4,20},{5,21},{6,22},{7,23},{8,24},{9,... | collective-permute-start | bytes 786440 | tf_op jit(solution)/shard_map/ppermute | solution.py:36
  143.5 12.8 %collective-permute-start.41 = (bf16[2,2,48,1024]{3,2,1,0:T(8,128)(2,1)S(1)}, bf16[2,2,48,1024]{3,2,1,0:T(8,128)(2,1)S(1)}, u32[]{:S(2)}, u32[]{:S(2)}) collective-permute-start(bf16[2,2,48,1024]{3,2,1,0:T(8,128)(2,1)S(1)} %slice_bitcast_fusion.16), channel_id=1, source_target_pairs={{0,1},{1,0},{2,6},{3,7},{4,5},{5,4},{6,2},{7,3},{8,9},{9,8},{10,14... | collective-permute-start | bytes 1179656 | tf_op jit(solution)/shard_map/ppermute | solution.py:36
  143.9 12.5 %collective-permute-start.42 = (bf16[2,2,48,1024]{3,2,1,0:T(8,128)(2,1)S(1)}, bf16[2,2,48,1024]{3,2,1,0:T(8,128)(2,1)S(1)}, u32[]{:S(2)}, u32[]{:S(2)}) collective-permute-start(bf16[2,2,48,1024]{3,2,1,0:T(8,128)(2,1)S(1)} %slice_bitcast_fusion.14), channel_id=1, source_target_pairs={{0,1},{1,0},{2,6},{3,7},{4,5},{5,4},{6,2},{7,3},{8,9},{9,8},{10,14... | collective-permute-start | bytes 1179656 | tf_op jit(solution)/shard_map/ppermute | solution.py:36
  162.6 15.6 %collective-permute-start.50 = (bf16[128,1024]{1,0:T(8,128)(2,1)S(1)}, bf16[128,1024]{1,0:T(8,128)(2,1)S(1)}, u32[]{:S(2)}, u32[]{:S(2)}) collective-permute-start(bf16[128,1024]{1,0:T(8,128)(2,1)S(1)} %fusion.8), channel_id=1, source_target_pairs={{0,16},{1,17},{2,18},{3,19},{4,20},{5,21},{6,22},{7,23},{8,24},{9,... | collective-permute-start | bytes 786440 | tf_op jit(solution)/shard_map/ppermute | solution.py:36
  166.7 14.0 %collective-permute-start.48 = (bf16[128,1024]{1,0:T(8,128)(2,1)S(1)}, bf16[128,1024]{1,0:T(8,128)(2,1)S(1)}, u32[]{:S(2)}, u32[]{:S(2)}) collective-permute-start(bf16[128,1024]{1,0:T(8,128)(2,1)S(1)} %fusion.16), channel_id=1, source_target_pairs={{0,8},{1,9},{2,10},{3,11},{4,12},{5,13},{6,14},{7,15},{8,0},{9,1},... | collective-permute-start | bytes 786440 | tf_op jit(solution)/shard_map/ppermute | solution.py:36
  (37 other events, 344.3 us)
